TPU v7x, 128 devices: a whole 4x4x4 slice. The times are simulated.
128 devices in a mesh: comp: 2 (over z_lo), gx: 8 (over x, core), gy: 8 (over y, z_hi).
Axes of the slice: x: 4, y: 4, z: 4 (z_hi: 2, z_lo: 2; z = z_hi * 2 + z_lo), core: 2. Of those that a mesh axis runs over, the one named last changes fastest.
Arguments:
- state: float32 [2, 16, 1024, 1024], P('comp', None, 'gx', 'gy'), may hold values from -6 to 6
- velocity: bfloat16 [2, 2, 16, 1024, 1024], P('comp', None, None, 'gx', 'gy'), may hold values from -0.5 to 0.5
- diffusivity: float32 [2, 16], P('comp'), may hold values from 0.02 to 0.2
- export_proj: float32 [2, 8, 16], P('comp'), may hold values from -1.5 to 1.5
- import_proj: float32 [2, 16, 8], P('comp'), may hold values from -2 to 2
- intersection_weights: bfloat16 [2, 1024, 8, 4, 128, 128], P('comp', 'gx', 'gy'), may hold values from -0.25 to 0.25
- recv_slots: int32 [2, 1024, 8, 4], P('comp', 'gx', 'gy'), may hold values from 0 to 1023, as said below
- send_slots: int32 [2, 8, 8, 64, 16], P(None, 'gx', 'gy'), may hold values from 0 to 127, as said below
- land: int32 [1024, 8], P('gx', 'gy'), may hold values 0 or 1
Outputs:
- new_state: float32 [2, 16, 1024, 1024], P('comp', None, 'gx', 'gy')
- imported: bfloat16 [2, 1024, 8, 1024], P('comp', 'gx', None, 'gy')
Inputs may be any that keep to these rules, and one draw needn't show every extreme that they name: `recv_slots`: entry p names the place, source device times 16 plus place, in the buffer from the other component; each destination device reads each place at most once; at most 16 of one destination device's tiles' references come from one source device, and for every destination device exactly 16 come from one source device. Source devices are numbered row-major over gx and gy. `send_slots`: entry [c, a, b, d, q] is the local block row that source device (a, b) of component c puts into place q of its buffer for destination device d of the other component; places that no destination reads hold 0.
All inputs are finite; a program needn't handle non-finite values. No bound on the sum of `land` on one device may be relied on, other than what follows from the above.
Results may differ from a plain program's by a relative error of at most 0.0049.
Values may be sent and summed in bfloat16 or wider, within the bound.
A program may use at most 128 MiB of HBM per device.

v0:
```python
import jax
import jax.numpy as jnp
from jax import lax
from jax.sharding import PartitionSpec as P

STEPS = 2


def padded_2(cells, sides, width):
    for axis, dim in sides:
        count = lax.axis_size(axis)
        ends = count - 1
        head = lax.slice_in_dim(cells, 0, width, axis=dim)
        tail = lax.slice_in_dim(cells, cells.shape[dim] - width, cells.shape[dim], axis=dim)
        cells = jnp.concatenate(
            [
                lax.ppermute(tail, axis, [(i, (i + 1) % count) for i in range(ends)]),
                cells,
                lax.ppermute(head, axis, [((i + 1) % count, i) for i in range(ends)]),
            ],
            axis=dim,
        )
    return cells


def advance(tracer, speeds, coeffs, wet_mask):
    padded = padded_2(tracer.astype(jnp.bfloat16), (("gx", 1), ("gy", 2)), 1).astype(tracer.dtype)
    row_down = padded[:, 2:, 1:-1]
    row_up = padded[:, :-2, 1:-1]
    col_right = padded[:, 1:-1, 2:]
    col_left = padded[:, 1:-1, :-2]
    spread = row_down + row_up + col_right + col_left - 4.0 * tracer
    carried = 0.5 * (
        speeds[0].astype(jnp.float32) * (row_down - row_up)
        + speeds[1].astype(jnp.float32) * (col_right - col_left)
    )
    return tracer + wet_mask * (coeffs[:, None, None] * spread - carried)


def per_device(
    state,
    velocity,
    diffusivity,
    export_proj,
    import_proj,
    intersection_weights,
    recv_slots,
    send_slots,
    land,
):
    highest = lax.Precision.HIGHEST
    section = lax.axis_index("comp")
    tracer = state[0]
    wet_tile = jnp.where(section == 0, jnp.ones(land.shape, jnp.float32), land.astype(jnp.float32))
    exports = (
        jnp.einsum("fl,lxy->xfy", export_proj[0], tracer, precision=highest) * wet_tile[:, :, None]
    ).astype(jnp.bfloat16)
    tables = send_slots[:, 0, 0]
    own_table = lax.dynamic_index_in_dim(tables, section, 0, keepdims=False)
    packed = exports[own_table]
    empty_half = jnp.zeros_like(packed)
    outgoing = jnp.where(
        section == 0,
        jnp.concatenate([empty_half, packed], axis=0),
        jnp.concatenate([packed, empty_half], axis=0),
    )
    arrived = lax.all_to_all(
        outgoing, ("comp", "gx", "gy"), split_axis=0, concat_axis=0, tiled=True
    )
    group_size = packed.shape[0]
    arrived = lax.dynamic_slice_in_dim(arrived, (1 - section) * group_size, group_size, 0)
    flat_slots = arrived.reshape(-1, exports.shape[1], exports.shape[2])
    sources = flat_slots[recv_slots[0, :, 0, :]]
    summed = lax.dot_general(
        sources,
        intersection_weights[0, :, 0],
        (((1, 3), (1, 3)), ((0,), (0,))),
        preferred_element_type=jnp.float32,
    )
    imported = (summed * wet_tile[:, :, None]).astype(jnp.bfloat16)
    wet_cells = wet_tile[None]
    for repeat in range(STEPS):
        tracer = advance(tracer, velocity[0], diffusivity[0], wet_cells)
    forcing = jnp.einsum(
        "lf,xfy->lxy", import_proj[0], imported.astype(jnp.float32), precision=highest
    )
    return ((tracer + wet_cells * forcing)[None], imported[None])


def solution(mesh):
    return jax.shard_map(
        per_device,
        mesh=mesh,
        in_specs=(
            P("comp", None, "gx", "gy"),
            P("comp", None, None, "gx", "gy"),
            P("comp", None),
            P("comp", None, None),
            P("comp", None, None),
            P("comp", "gx", "gy", None, None, None),
            P("comp", "gx", "gy", None),
            P(None, "gx", "gy", None, None),
            P("gx", "gy"),
        ),
        out_specs=(P("comp", None, "gx", "gy"), P("comp", "gx", None, "gy")),
        check_vma=False,
    )
```

profile of v0, /device:TPU:30, one launch (start us, length us, event | category | flops | bytes accessed | tf_op | source)
XLA Modules:
  0.0 128.2 jit_solution(9461427223233699347)
XLA Ops:
  2.2 2.4 %fusion.15 = bf16[128,8,128]{2,1,0:T(8,128)(2,1)S(1)} fusion(f32[1,16,128,128]{3,2,1,0:T(8,128)} %param.9, f32[128]{0:T(128)S(1)} %fusion.32, f32[1,8,16]{2,1,0:T(8,128)} %param.12), kind=kOutput, calls=%fused_computation.18 | convolution fusion | flops 25427968 | bytes 1311744 | tf_op jit(solution)/shard_map/fl,lxy->xfy/dot_general | solution.py:56
  4.6 3.3 %gather_fusion = bf16[1024,8,128]{2,1,0:T(8,128)(2,1)S(1)} fusion(bf16[128,8,128]{2,1,0:T(8,128)(2,1)S(1)} %fusion.15, s32[1024]{0:T(1024)S(1)} %broadcast_clamp_fusion), kind=kCustom, calls=%fused_computation | custom fusion | bytes 4198400 | tf_op jit(solution)/shard_map/gather | solution.py:60
  8.0 2.3 %pad_select_fusion = bf16[128,16,8,128]{3,2,1,0:T(8,128)(2,1)} fusion(bf16[64,16,8,128]{3,2,1,0:T(8,128)(2,1)S(1)} %bitcast.81, pred[]{:T(512)S(6)} %eq.4), kind=kLoop, calls=%fused_computation.4 | loop fusion | flops 2097152 | bytes 6291457 | tf_op jit(solution)/shard_map/jit(_where)/select_n | solution.py:62
  10.3 10.7 %all-to-all-start = ((bf16[128,16,8,128]{3,2,1,0:T(8,128)(2,1)}), bf16[128,16,8,128]{3,2,1,0:T(8,128)(2,1)}, u32[]{:S(2)}, u32[]{:S(2)}) async-start(bf16[128,16,8,128]{3,2,1,0:T(8,128)(2,1)} %pad_select_fusion), calls=%async_computation | async-start | bytes 8388608 | tf_op jit(solution)/shard_map/all_to_all | solution.py:67
  21.6 2.5 %collective-permute-start.1 = (bf16[16,1,128]{2,0,1:T(8,128)(2,1)S(1)}, bf16[16,1,128]{2,0,1:T(8,128)(2,1)S(1)}, u32[]{:S(2)}, u32[]{:S(2)}) collective-permute-start(bf16[16,1,128]{2,0,1:T(8,128)(2,1)S(1)} %get-tuple-element.21), channel_id=1, source_target_pairs={{8,0},{16,8},{24,16},{32,24},{40,32},{48,40},{56,48},{9,1},{17,9},... | collective-permute-start | bytes 12296 | tf_op jit(solution)/shard_map/ppermute | solution.py:19
  24.1 1.9 %collective-permute-start = (bf16[16,1,128]{2,0,1:T(8,128)(2,1)S(1)}, bf16[16,1,128]{2,0,1:T(8,128)(2,1)S(1)}, u32[]{:S(2)}, u32[]{:S(2)}) collective-permute-start(bf16[16,1,128]{2,0,1:T(8,128)(2,1)S(1)} %get-tuple-element.20), channel_id=1, source_target_pairs={{0,8},{8,16},{16,24},{24,32},{32,40},{40,48},{48,56},{1,9},{9,17},... | collective-permute-start | bytes 12296 | tf_op jit(solution)/shard_map/ppermute | solution.py:17
  26.0 39.5 %collective-permute-done.1 = bf16[16,1,128]{2,0,1:T(8,128)(2,1)S(1)} collective-permute-done((bf16[16,1,128]{2,0,1:T(8,128)(2,1)S(1)}, bf16[16,1,128]{2,0,1:T(8,128)(2,1)S(1)}, u32[]{:S(2)}, u32[]{:S(2)}) %collective-permute-start.1) | collective-permute-done | bytes 4128 | tf_op jit(solution)/shard_map/ppermute | solution.py:19
  67.1 5.6 %collective-permute-start.3 = (bf16[16,130,1]{1,0,2:T(8,128)(2,1)S(1)}, bf16[16,130,1]{1,0,2:T(8,128)(2,1)S(1)}, u32[]{:S(2)}, u32[]{:S(2)}) collective-permute-start(bf16[16,130,1]{1,0,2:T(8,128)(2,1)S(1)} %copy.28), channel_id=1, source_target_pairs={{1,0},{2,1},{3,2},{4,3},{5,4},{6,5},{7,6},{9,8},{10,9},{11,10},{12... | collective-permute-start | bytes 12488 | tf_op jit(solution)/shard_map/ppermute | solution.py:19
  73.3 1.9 %collective-permute-start.2 = (bf16[16,130,1]{1,0,2:T(8,128)(2,1)S(1)}, bf16[16,130,1]{1,0,2:T(8,128)(2,1)S(1)}, u32[]{:S(2)}, u32[]{:S(2)}) collective-permute-start(bf16[16,130,1]{1,0,2:T(8,128)(2,1)S(1)} %copy.27), channel_id=1, source_target_pairs={{0,1},{1,2},{2,3},{3,4},{4,5},{5,6},{6,7},{8,9},{9,10},{10,11},{11... | collective-permute-start | bytes 12488 | tf_op jit(solution)/shard_map/ppermute | solution.py:17
  75.2 2.1 %fusion.35 = (bf16[1,1,16,128,128]{4,3,2,1,0:T(8,128)(2,1)S(1)}, bf16[1,1,16,128,128]{4,3,2,1,0:T(8,128)(2,1)}) fusion(bf16[1,2,16,128,128]{4,3,2,1,0:T(8,128)(2,1)} %param.10), kind=kLoop, calls=%fused_computation.51 | loop fusion | bytes 2097152 | tf_op jit(solution)/shard_map/slice | solution.py:34
  77.9 3.3 %collective-permute-done.2 = bf16[16,130,1]{1,0,2:T(8,128)(2,1)S(1)} collective-permute-done((bf16[16,130,1]{1,0,2:T(8,128)(2,1)S(1)}, bf16[16,130,1]{1,0,2:T(8,128)(2,1)S(1)}, u32[]{:S(2)}, u32[]{:S(2)}) %collective-permute-start.2) | collective-permute-done | bytes 4192 | tf_op jit(solution)/shard_map/ppermute | solution.py:17
  82.8 2.7 %fusion.33 = (bf16[16,128,128]{2,0,1:T(8,128)(2,1)S(1)}, f32[16,128,128]{2,0,1:T(8,128)}) fusion(bf16[1,1,16,128,128]{4,3,2,1,0:T(8,128)(2,1)S(1)} %copy-done.4, bf16[1,1,16,128,128]{4,3,2,1,0:T(8,128)(2,1)S(1)} %get-tuple-element.12, f32[16,130,130]{2,0,1:T(8,128)S(1)} %maximum_convert_fusion, f32[16]{0:T(128)S(1)} %bitcast.88, f32[128]{0:T(128)S(1)} %fusion.32, ...), kind=kLoop, calls=%fused_computation.50 | loop fusion | flops 4718592 | bytes 7864896 | tf_op jit(solution)/shard_map/convert_element_type | solution.py:27
  85.6 2.6 %collective-permute-start.5 = (bf16[16,1,128]{2,0,1:T(8,128)(2,1)S(1)}, bf16[16,1,128]{2,0,1:T(8,128)(2,1)S(1)}, u32[]{:S(2)}, u32[]{:S(2)}) collective-permute-start(bf16[16,1,128]{2,0,1:T(8,128)(2,1)S(1)} %get-tuple-element.19), channel_id=1, source_target_pairs={{8,0},{16,8},{24,16},{32,24},{40,32},{48,40},{56,48},{9,1},{17,9},... | collective-permute-start | bytes 12296 | tf_op jit(solution)/shard_map/ppermute | solution.py:19
  88.2 1.9 %collective-permute-start.4 = (bf16[16,1,128]{2,0,1:T(8,128)(2,1)S(1)}, bf16[16,1,128]{2,0,1:T(8,128)(2,1)S(1)}, u32[]{:S(2)}, u32[]{:S(2)}) collective-permute-start(bf16[16,1,128]{2,0,1:T(8,128)(2,1)S(1)} %get-tuple-element.18), channel_id=1, source_target_pairs={{0,8},{8,16},{16,24},{24,32},{32,40},{40,48},{48,56},{1,9},{9,17},... | collective-permute-start | bytes 12296 | tf_op jit(solution)/shard_map/ppermute | solution.py:17
  90.4 2.7 %collective-permute-done.4 = bf16[16,1,128]{2,0,1:T(8,128)(2,1)S(1)} collective-permute-done((bf16[16,1,128]{2,0,1:T(8,128)(2,1)S(1)}, bf16[16,1,128]{2,0,1:T(8,128)(2,1)S(1)}, u32[]{:S(2)}, u32[]{:S(2)}) %collective-permute-start.4) | collective-permute-done | bytes 4128 | tf_op jit(solution)/shard_map/ppermute | solution.py:17
  94.0 3.9 %collective-permute-start.7 = (bf16[16,130,1]{1,0,2:T(8,128)(2,1)S(1)}, bf16[16,130,1]{1,0,2:T(8,128)(2,1)S(1)}, u32[]{:S(2)}, u32[]{:S(2)}) collective-permute-start(bf16[16,130,1]{1,0,2:T(8,128)(2,1)S(1)} %copy.34), channel_id=1, source_target_pairs={{1,0},{2,1},{3,2},{4,3},{5,4},{6,5},{7,6},{9,8},{10,9},{11,10},{12... | collective-permute-start | bytes 12488 | tf_op jit(solution)/shard_map/ppermute | solution.py:19
  98.4 3.6 %collective-permute-start.6 = (bf16[16,130,1]{1,0,2:T(8,128)(2,1)S(1)}, bf16[16,130,1]{1,0,2:T(8,128)(2,1)S(1)}, u32[]{:S(2)}, u32[]{:S(2)}) collective-permute-start(bf16[16,130,1]{1,0,2:T(8,128)(2,1)S(1)} %copy.33), channel_id=1, source_target_pairs={{0,1},{1,2},{2,3},{3,4},{4,5},{5,6},{6,7},{8,9},{9,10},{10,11},{11... | collective-permute-start | bytes 12488 | tf_op jit(solution)/shard_map/ppermute | solution.py:17
  102.6 3.7 %collective-permute-done.6 = bf16[16,130,1]{1,0,2:T(8,128)(2,1)S(1)} collective-permute-done((bf16[16,130,1]{1,0,2:T(8,128)(2,1)S(1)}, bf16[16,130,1]{1,0,2:T(8,128)(2,1)S(1)}, u32[]{:S(2)}, u32[]{:S(2)}) %collective-permute-start.6) | collective-permute-done | bytes 4192 | tf_op jit(solution)/shard_map/ppermute | solution.py:17
  106.9 2.0 %maximum_convert_fusion.1 = f32[16,130,130]{2,0,1:T(8,128)} fusion(bf16[16,130,1]{2,0,1:T(8,128)(2,1)S(1)} %copy.36, bf16[16,1,128]{2,0,1:T(8,128)(2,1)S(1)} %collective-permute-done.5, bf16[16,128,128]{2,0,1:T(8,128)(2,1)S(1)} %get-tuple-element.10, bf16[16,1,128]{2,0,1:T(8,128)(2,1)S(1)} %collective-permute-done.4, bf16[16,130,1]{2,0,1:T(8,128)(2,1)S(1)} %copy.35), kind=kLoop, calls=%fused_computation.20 | loop fusion | flops 2704000 | bytes 1622400 | tf_op jit(solution)/shard_map/convert_element_type | solution.py:27
  108.9 1.7 %constant_dynamic-slice_fusion = bf16[64,16,8,128]{3,2,1,0:T(8,128)(2,1)S(1)} fusion(bf16[128,16,8,128]{3,2,1,0:T(8,128)(2,1)} %all-to-all-done, s32[]{:T(128)S(6)} %select_n.49), kind=kLoop, calls=%fused_computation.49 | loop fusion | bytes 4194308 | tf_op jit(solution)/shard_map/dynamic_slice | solution.py:71
  110.7 1.8 %gather_fusion.1 = bf16[512,8,128]{2,1,0:T(8,128)(2,1)S(1)} fusion(bf16[1024,8,128]{2,1,0:T(8,128)(2,1)S(1)} %bitcast.85, s32[1024]{0:T(1024)S(1)} %pad_clamp_fusion), kind=kCustom, calls=%fused_computation.1 | custom fusion | bytes 2099200 | tf_op jit(solution)/shard_map/gather | solution.py:73
  112.5 8.4 %fusion.12 = bf16[128,8,128]{2,1,0:T(8,128)(2,1)S(1)} fusion(bf16[128,4,8,128]{3,2,1,0:T(8,128)(2,1)S(1)} %bitcast.86, bf16[1,128,1,4,128,128]{5,4,3,2,1,0:T(8,128)(2,1)} %param.14, f32[128]{0:T(128)S(1)} %fusion.32), kind=kOutput, calls=%fused_computation.17 | convolution fusion | flops 134479872 | bytes 18088448 | tf_op jit(solution)/shard_map/dot_general | solution.py:74
  120.9 5.9 %fusion.4 = f32[1,16,128,128]{3,1,2,0:T(8,128)S(1)} fusion(bf16[128,8,128]{2,1,0:T(8,128)(2,1)S(1)} %fusion.12, f32[16,128,128]{2,0,1:T(8,128)S(1)} %copy-done.6, f32[16,130,130]{2,0,1:T(8,128)} %maximum_convert_fusion.1, f32[128]{0:T(128)S(1)} %fusion.32, f32[16]{0:T(128)S(1)} %bitcast.89, bf16[1,1,16,128,128]{4,3,2,1,0:T(8,128)(2,1)S(1)} %copy-done.3, ...), kind=kOutput, calls=%fused_computation.8 | convolution fusion | flops 30146560 | bytes 7607808 | tf_op jit(solution)/shard_map/lf,xfy->lxy/dot_general | solution.py:84
  126.9 1.3 %copy.39 = f32[1,16,128,128]{3,2,1,0:T(8,128)} copy(f32[1,16,128,128]{3,1,2,0:T(8,128)S(1)} %fusion.4) | data formatting | bytes 2097152
  (50 shorter events, 9.2 us)
Async XLA Ops:
  0.6 120.3 %copy-start = (f32[1,16,8]{1,2,0:T(8,128)S(1)}, f32[1,16,8]{1,2,0:T(8,128)}, u32[]{:S(2)}) copy-start(f32[1,16,8]{1,2,0:T(8,128)} %param.13) | copy-start | bytes 1540
  10.3 10.7 %copy-start.1 = (f32[1,16,128,128]{3,2,1,0:T(8,128)S(1)}, f32[1,16,128,128]{3,2,1,0:T(8,128)}, u32[]{:S(2)}) copy-start(f32[1,16,128,128]{3,2,1,0:T(8,128)} %param.9) | copy-start | bytes 3145732
  10.3 98.7 %all-to-all-start = ((bf16[128,16,8,128]{3,2,1,0:T(8,128)(2,1)}), bf16[128,16,8,128]{3,2,1,0:T(8,128)(2,1)}, u32[]{:S(2)}, u32[]{:S(2)}) async-start(bf16[128,16,8,128]{3,2,1,0:T(8,128)(2,1)} %pad_select_fusion), calls=%async_computation | async-start | bytes 8388608 | tf_op jit(solution)/shard_map/all_to_all | solution.py:67
  21.6 44.0 %collective-permute-start.1 = (bf16[16,1,128]{2,0,1:T(8,128)(2,1)S(1)}, bf16[16,1,128]{2,0,1:T(8,128)(2,1)S(1)}, u32[]{:S(2)}, u32[]{:S(2)}) collective-permute-start(bf16[16,1,128]{2,0,1:T(8,128)(2,1)S(1)} %get-tuple-element.21), channel_id=1, source_target_pairs={{8,0},{16,8},{24,16},{32,24},{40,32},{48,40},{56,48},{9,1},{17,9},... | collective-permute-start | bytes 12296 | tf_op jit(solution)/shard_map/ppermute | solution.py:19
  24.1 42.1 %collective-permute-start = (bf16[16,1,128]{2,0,1:T(8,128)(2,1)S(1)}, bf16[16,1,128]{2,0,1:T(8,128)(2,1)S(1)}, u32[]{:S(2)}, u32[]{:S(2)}) collective-permute-start(bf16[16,1,128]{2,0,1:T(8,128)(2,1)S(1)} %get-tuple-element.20), channel_id=1, source_target_pairs={{0,8},{8,16},{16,24},{24,32},{32,40},{40,48},{48,56},{1,9},{9,17},... | collective-permute-start | bytes 12296 | tf_op jit(solution)/shard_map/ppermute | solution.py:17
  67.1 10.2 %collective-permute-start.3 = (bf16[16,130,1]{1,0,2:T(8,128)(2,1)S(1)}, bf16[16,130,1]{1,0,2:T(8,128)(2,1)S(1)}, u32[]{:S(2)}, u32[]{:S(2)}) collective-permute-start(bf16[16,130,1]{1,0,2:T(8,128)(2,1)S(1)} %copy.28), channel_id=1, source_target_pairs={{1,0},{2,1},{3,2},{4,3},{5,4},{6,5},{7,6},{9,8},{10,9},{11,10},{12... | collective-permute-start | bytes 12488 | tf_op jit(solution)/shard_map/ppermute | solution.py:19
  73.3 7.9 %collective-permute-start.2 = (bf16[16,130,1]{1,0,2:T(8,128)(2,1)S(1)}, bf16[16,130,1]{1,0,2:T(8,128)(2,1)S(1)}, u32[]{:S(2)}, u32[]{:S(2)}) collective-permute-start(bf16[16,130,1]{1,0,2:T(8,128)(2,1)S(1)} %copy.27), channel_id=1, source_target_pairs={{0,1},{1,2},{2,3},{3,4},{4,5},{5,6},{6,7},{8,9},{9,10},{10,11},{11... | collective-permute-start | bytes 12488 | tf_op jit(solution)/shard_map/ppermute | solution.py:17
  77.3 5.1 %copy-start.2 = (bf16[1,1,16,128,128]{4,3,2,1,0:T(8,128)(2,1)}, bf16[1,1,16,128,128]{4,3,2,1,0:T(8,128)(2,1)S(1)}, u32[]{:S(2)}) copy-start(bf16[1,1,16,128,128]{4,3,2,1,0:T(8,128)(2,1)S(1)} %get-tuple-element.12) | copy-start | bytes 1572868
  77.9 4.5 %copy-start.9 = (f32[1,16]{1,0:T(1,128)S(1)}, f32[1,16]{1,0:T(1,128)}, u32[]{:S(2)}) copy-start(f32[1,16]{1,0:T(1,128)} %param.11) | copy-start | bytes 196
  81.8 1.0 copy-start.4
  82.8 7.3 %copy-start.8 = (s32[1,128,1,4]{1,3,2,0:T(4,128)S(1)}, s32[1,128,1,4]{1,3,2,0:T(4,128)}, u32[]{:S(2)}) copy-start(s32[1,128,1,4]{1,3,2,0:T(4,128)} %param.15) | copy-start | bytes 6148
  85.6 4.8 %collective-permute-start.5 = (bf16[16,1,128]{2,0,1:T(8,128)(2,1)S(1)}, bf16[16,1,128]{2,0,1:T(8,128)(2,1)S(1)}, u32[]{:S(2)}, u32[]{:S(2)}) collective-permute-start(bf16[16,1,128]{2,0,1:T(8,128)(2,1)S(1)} %get-tuple-element.19), channel_id=1, source_target_pairs={{8,0},{16,8},{24,16},{32,24},{40,32},{48,40},{56,48},{9,1},{17,9},... | collective-permute-start | bytes 12296 | tf_op jit(solution)/shard_map/ppermute | solution.py:19
  88.2 4.9 %collective-permute-start.4 = (bf16[16,1,128]{2,0,1:T(8,128)(2,1)S(1)}, bf16[16,1,128]{2,0,1:T(8,128)(2,1)S(1)}, u32[]{:S(2)}, u32[]{:S(2)}) collective-permute-start(bf16[16,1,128]{2,0,1:T(8,128)(2,1)S(1)} %get-tuple-element.18), channel_id=1, source_target_pairs={{0,8},{8,16},{16,24},{24,32},{32,40},{40,48},{48,56},{1,9},{9,17},... | collective-permute-start | bytes 12296 | tf_op jit(solution)/shard_map/ppermute | solution.py:17
  94.0 8.1 %collective-permute-start.7 = (bf16[16,130,1]{1,0,2:T(8,128)(2,1)S(1)}, bf16[16,130,1]{1,0,2:T(8,128)(2,1)S(1)}, u32[]{:S(2)}, u32[]{:S(2)}) collective-permute-start(bf16[16,130,1]{1,0,2:T(8,128)(2,1)S(1)} %copy.34), channel_id=1, source_target_pairs={{1,0},{2,1},{3,2},{4,3},{5,4},{6,5},{7,6},{9,8},{10,9},{11,10},{12... | collective-permute-start | bytes 12488 | tf_op jit(solution)/shard_map/ppermute | solution.py:19
  98.4 7.9 %collective-permute-start.6 = (bf16[16,130,1]{1,0,2:T(8,128)(2,1)S(1)}, bf16[16,130,1]{1,0,2:T(8,128)(2,1)S(1)}, u32[]{:S(2)}, u32[]{:S(2)}) collective-permute-start(bf16[16,130,1]{1,0,2:T(8,128)(2,1)S(1)} %copy.33), channel_id=1, source_target_pairs={{0,1},{1,2},{2,3},{3,4},{4,5},{5,6},{6,7},{8,9},{9,10},{10,11},{11... | collective-permute-start | bytes 12488 | tf_op jit(solution)/shard_map/ppermute | solution.py:17
  112.5 8.4 %copy-start.3 = (bf16[1,1,16,128,128]{4,3,2,1,0:T(8,128)(2,1)S(1)}, bf16[1,1,16,128,128]{4,3,2,1,0:T(8,128)(2,1)}, u32[]{:S(2)}) copy-start(bf16[1,1,16,128,128]{4,3,2,1,0:T(8,128)(2,1)} %copy-done.2) | copy-start | bytes 1572868
  112.5 8.4 %copy-start.5 = (bf16[1,1,16,128,128]{4,3,2,1,0:T(8,128)(2,1)S(1)}, bf16[1,1,16,128,128]{4,3,2,1,0:T(8,128)(2,1)}, u32[]{:S(2)}) copy-start(bf16[1,1,16,128,128]{4,3,2,1,0:T(8,128)(2,1)} %get-tuple-element.13) | copy-start | bytes 1572868
  112.5 8.4 %copy-start.6 = (f32[16,128,128]{2,0,1:T(8,128)S(1)}, f32[16,128,128]{2,0,1:T(8,128)}, u32[]{:S(2)}) copy-start(f32[16,128,128]{2,0,1:T(8,128)} %get-tuple-element.11) | copy-start | bytes 3145732
  120.9 6.0 %copy-start.7 = (bf16[128,8,128]{2,1,0:T(8,128)(2,1)}, bf16[128,8,128]{2,1,0:T(8,128)(2,1)S(1)}, u32[]{:S(2)}) copy-start(bf16[128,8,128]{2,1,0:T(8,128)(2,1)S(1)} %fusion.12) | copy-start | bytes 786436
where the time goes:
time: 129 us; the launch traced here: 128 us
  waiting for transfers between devices  50 us (39%)
  starting transfers between devices  34.7 us (27%)
  matrix products  16.8 us (13%)
  local copies, waits for them, and re-layouts  16.6 us (13%)
  other arithmetic  9.15 us (7%)
    ppermute x4, waiting for transfers between devices, padded_2(): lax.ppermute(head, axis, [((i + 1) % count, i) for i in range(ends)])  39.6 us
    ppermute x4, starting transfers between devices, padded_2(): lax.ppermute(head, axis, [((i + 1) % count, i) for i in range(ends)])  14.6 us
    all_to_all x1, starting transfers between devices, per_device(): lax.all_to_all(outgoing, ('comp', 'gx', 'gy'), split_axis=0, concat_axis=...  10.7 us
    ppermute x4, waiting for transfers between devices, padded_2(): lax.ppermute(tail, axis, [(i, (i + 1) % count) for i in range(ends)])  10.4 us
    ppermute x4, starting transfers between devices, padded_2(): lax.ppermute(tail, axis, [(i, (i + 1) % count) for i in range(ends)])  9.36 us
    dot_general x1, matrix products, per_device(): lax.dot_general(sources, intersection_weights[0, :, 0], (((1, 3), (1, 3))...  8.37 us
    dot_general x1, matrix products, per_device(): jnp.einsum('lf,xfy->lxy', import_proj[0], imported.astype(jnp.float32), p...  5.94 us
    gather x1, local copies, waits for them, and re-layouts, per_device(): packed = exports[own_table]  3.31 us
  transfers between devices with their start and end apart: 9, of which 5 were waited for; matrix products, arithmetic and copies ran while one was open for 10% of the time, Pallas kernels for 0%

commit v1 on v0

v1 whole, which is shorter than its diff:
```python
import functools

import jax
import jax.numpy as jnp
from jax import lax
from jax.experimental import pallas as pl
from jax.experimental.pallas import tpu as pltpu
from jax.sharding import PartitionSpec as P

MESH = pl.DeviceIdType.MESH
F32 = jnp.float32
BF16 = jnp.bfloat16

LEV, FLD, K = 16, 8, 4
ROWS, TILE = 128, 128
N_GX, N_GY = 8, 8
GROUP, CAP = 64, 16
TOP = 8
PADDED = ROWS + 2 * TOP
W_PARTS = 8
FIRST, SECOND = 12, 44


def partner(turn, gx, gy):
    x = lax.rem(lax.div(gx, 2) + lax.div(turn, 16), 4)
    core = lax.rem(lax.rem(gx, 2) + lax.rem(lax.div(turn, 8), 2), 2)
    y = lax.rem(lax.div(gy, 2) + lax.rem(lax.div(turn, 2), 4), 4)
    high = lax.rem(lax.rem(gy, 2) + lax.rem(turn, 2), 2)
    return x * 2 + core, y * 2 + high


def exchange_kernel(
    state_hbm, vel_hbm, w_hbm, proj, diff, table, land, land_row,
    arrived, tracer, w_out,
    ta, tb, vel, ex, buf, halo_out, halo_in, wet,
    sem_state, sem_vel, sem_w, sem_send, sem_recv, sem_hs, sem_hr,
):
    comp, gx, gy = lax.axis_index("comp"), lax.axis_index("gx"), lax.axis_index("gy")
    other = 1 - comp
    me = gx * N_GY + gy
    up, down = lax.rem(gx + N_GX - 1, N_GX), lax.rem(gx + 1, N_GX)
    left, right = lax.rem(gy + N_GY - 1, N_GY), lax.rem(gy + 1, N_GY)
    beside = ((comp, up, gy), (comp, down, gy), (comp, gx, left), (comp, gx, right))

    interior = pl.ds(TOP, ROWS)
    get_state = pltpu.make_async_copy(state_hbm, ta.at[:, interior], sem_state)
    get_state.start()
    get_vel = pltpu.make_async_copy(vel_hbm, vel, sem_vel)
    get_vel.start()

    barrier = pltpu.get_barrier_semaphore()
    for device in beside:
        pl.semaphore_signal(barrier, inc=1, device_id=device, device_id_type=MESH)

    def greet(d, carry):
        pl.semaphore_signal(
            barrier, inc=1, device_id=(other, lax.div(d, N_GY), lax.rem(d, N_GY)), device_id_type=MESH
        )
        return carry

    lax.fori_loop(0, GROUP, greet, 0)

    part = w_hbm.shape[0] // W_PARTS

    def get_w(i):
        rows = pl.ds(i * part, part)
        return pltpu.make_async_copy(w_hbm.at[rows], w_out.at[rows], sem_w.at[i])

    for i in range(W_PARTS):
        get_w(i).start()

    row_wet = jnp.where(comp == 0, jnp.ones((1, TILE), F32), land_row[...].astype(F32))
    wet[...] = jnp.transpose(jnp.broadcast_to(row_wet, (ROWS, TILE)))

    columns = [jnp.broadcast_to(proj[:, l : l + 1], (FLD, TILE)) for l in range(LEV)]
    get_state.wait()

    def export(i, carry):
        for j in range(4):
            x = i * 4 + j
            total = columns[0] * ta[0, pl.ds(TOP + x, 1), :]
            for l in range(1, LEV):
                total += columns[l] * ta[l, pl.ds(TOP + x, 1), :]
            ex[x] = total * jnp.where(comp == 0, 1.0, land[0, x].astype(F32))
        return carry

    lax.fori_loop(0, ROWS // 4, export, 0)
    pl.semaphore_wait(barrier, GROUP + 4)

    def serve(turn, carry):
        to_x, to_y = partner(turn, gx, gy)
        d = to_x * N_GY + to_y
        for q in range(CAP):
            buf[turn * CAP + q] = ex[table[comp, q, d]].astype(BF16)
        pltpu.make_async_remote_copy(
            src_ref=buf.at[pl.ds(turn * CAP, CAP)],
            dst_ref=arrived.at[pl.ds(me * CAP, CAP)],
            send_sem=sem_send,
            recv_sem=sem_recv,
            device_id=(other, to_x, to_y),
            device_id_type=MESH,
        ).start()
        return carry

    def pick(l):
        r = lax.broadcasted_iota(jnp.int32, (2 * LEV, TILE), 0)
        c = lax.broadcasted_iota(jnp.int32, (2 * LEV, TILE), 1)
        hit = ((r == l) & (c == 0)) | ((r == LEV + l) & (c == TILE - 1))
        return jnp.where(hit, 1.0, 0.0).astype(BF16)

    def halo_copy(turn, side):
        return pltpu.make_async_remote_copy(
            src_ref=halo_out.at[turn, side],
            dst_ref=halo_in.at[turn, side],
            send_sem=sem_hs.at[turn, side],
            recv_sem=sem_hr.at[turn, side],
            device_id=beside[side],
            device_id_type=MESH,
        )

    def send_halo(turn, t):
        flat = t.reshape(LEV * PADDED, TILE)
        halo_out[turn, 0] = flat[pl.ds(TOP, LEV, stride=PADDED), :].astype(BF16)
        halo_out[turn, 1] = flat[pl.ds(TOP + ROWS - 1, LEV, stride=PADDED), :].astype(BF16)

        def add(l, total):
            return total + lax.dot_general(
                pick(l), t[l, interior, :].astype(BF16), (((1,), (1,)), ((), ())), preferred_element_type=F32
            )

        edges = lax.fori_loop(0, LEV, add, jnp.zeros((2 * LEV, TILE), F32)).astype(BF16)
        halo_out[turn, 2] = edges[:LEV]
        halo_out[turn, 3] = edges[LEV:]
        for side in range(4):
            halo_copy(turn, side).start()

    def take_halo(turn, t):
        for side in range(4):
            halo_copy(turn, side).wait_recv()
        flat = t.reshape(LEV * PADDED, TILE)
        rows = [halo_in[turn, side].astype(F32) for side in range(4)]
        flat[pl.ds(TOP + ROWS, LEV, stride=PADDED), :] = jnp.where(gx < N_GX - 1, rows[0], 0.0)
        flat[pl.ds(TOP - 1, LEV, stride=PADDED), :] = jnp.where(gx > 0, rows[1], 0.0)
        last = jnp.where(gy < N_GY - 1, rows[2], 0.0)
        first = jnp.where(gy > 0, rows[3], 0.0)
        return jnp.transpose(jnp.concatenate([first, last], axis=0)).astype(BF16)

    def advance(t, edges, put):
        lane = lax.broadcasted_iota(jnp.int32, (ROWS, TILE), 1)

        def level(l, carry):
            mid = t[l, interior, :]
            above, below = t[l, pl.ds(TOP - 1, ROWS), :], t[l, pl.ds(TOP + 1, ROWS), :]
            sides = jnp.dot(edges, pick(l), preferred_element_type=F32)
            before = jnp.where(lane == 0, sides, pltpu.roll(mid, 1, 1))
            after = jnp.where(lane == TILE - 1, sides, pltpu.roll(mid, TILE - 1, 1))
            spread = above + below + before + after - 4.0 * mid
            carried = 0.5 * (
                vel[0, l].astype(F32) * (below - above) + vel[1, l].astype(F32) * (after - before)
            )
            put(l, mid + wet[...] * (diff[0, l] * spread - carried))
            return carry

        lax.fori_loop(0, LEV, level, 0)

    def put_tb(l, value):
        tb[l, interior, :] = value

    def put_tracer(l, value):
        tracer[l] = value

    lax.fori_loop(0, FIRST, serve, 0)
    send_halo(0, ta)
    lax.fori_loop(FIRST, SECOND, serve, 0)
    edges = take_halo(0, ta)
    get_vel.wait()
    advance(ta, edges, put_tb)
    send_halo(1, tb)
    lax.fori_loop(SECOND, GROUP, serve, 0)
    edges = take_halo(1, tb)
    advance(tb, edges, put_tracer)

    for i in range(W_PARTS):
        get_w(i).wait()
    for turn in range(2):
        for side in range(4):
            halo_copy(turn, side).wait_send()
    pltpu.make_async_copy(buf, buf, sem_send).wait()
    pltpu.make_async_copy(arrived, arrived, sem_recv).wait()


def remap_kernel(chunk, recv, land, ip, w, arrived, tracer, new_hbm, imp_hbm, new, imp, spread, sem_out):
    comp = lax.axis_index("comp")

    def out_copies(i):
        rows = pl.ds(pl.multiple_of(i * chunk, chunk), chunk)
        return (
            pltpu.make_async_copy(new.at[:, rows], new_hbm.at[:, rows], sem_out.at[0, i]),
            pltpu.make_async_copy(imp.at[rows], imp_hbm.at[rows], sem_out.at[1, i]),
        )

    for f in range(FLD):
        for l in range(LEV):
            spread[f, l : l + 1, :] = jnp.full((1, TILE), ip[f, l], F32)
    tracer_rows = tracer.reshape(LEV * ROWS, TILE)
    new_rows = new.reshape(LEV * ROWS, TILE)

    def step(i, carry):
        for j in range(chunk):
            x = i * chunk + j
            wet = jnp.where(comp == 0, 1.0, land[0, x].astype(F32))
            source = jnp.concatenate([arrived[recv[k, x]] for k in range(K)], axis=1)
            weights = jnp.concatenate([w[x, k] for k in range(K)], axis=1)
            summed = lax.dot_general(source, weights, (((1,), (1,)), ((), ())), preferred_element_type=F32)
            got = (summed * wet).astype(BF16)
            imp[x] = got
            got = got.astype(F32)
            force = spread[0] * got[0:1, :]
            for f in range(1, FLD):
                force += spread[f] * got[f : f + 1, :]
            rows = pl.ds(x, LEV, stride=ROWS)
            new_rows[rows, :] = tracer_rows[rows, :] + wet * force
        for copy in out_copies(i):
            copy.start()
        return carry

    def drain(i, carry):
        for copy in out_copies(i):
            copy.wait()
        return carry

    lax.fori_loop(0, ROWS // chunk, step, 0)
    lax.fori_loop(0, ROWS // chunk, drain, 0)


ANY = pl.BlockSpec(memory_space=pl.ANY)
HBM = pl.BlockSpec(memory_space=pltpu.HBM)
VMEM = pl.BlockSpec(memory_space=pltpu.VMEM)
SMEM = pl.BlockSpec(memory_space=pltpu.SMEM)


def exchange(state, velocity, weights, proj, diff, table, land):
    dma = pltpu.SemaphoreType.DMA
    return pl.pallas_call(
        exchange_kernel,
        name="exchange",
        out_shape=(
            pltpu.VMEM((GROUP * CAP, FLD, TILE), BF16),
            pltpu.VMEM((LEV, ROWS, TILE), F32),
            pltpu.VMEM((ROWS, K, TILE, TILE), BF16),
        ),
        in_specs=[HBM, HBM, HBM, VMEM, SMEM, SMEM, SMEM, VMEM],
        out_specs=(VMEM, VMEM, VMEM),
        scratch_shapes=[
            pltpu.VMEM((LEV, PADDED, TILE), F32),
            pltpu.VMEM((LEV, PADDED, TILE), F32),
            pltpu.VMEM((2, LEV, ROWS, TILE), BF16),
            pltpu.VMEM((ROWS, FLD, TILE), F32),
            pltpu.VMEM((GROUP * CAP, FLD, TILE), BF16),
            pltpu.VMEM((2, 4, LEV, TILE), BF16),
            pltpu.VMEM((2, 4, LEV, TILE), BF16),
            pltpu.VMEM((ROWS, TILE), F32),
            dma,
            dma,
            dma((W_PARTS,)),
            dma,
            dma,
            dma((2, 4)),
            dma((2, 4)),
        ],
        compiler_params=pltpu.CompilerParams(collective_id=0, has_side_effects=True, vmem_limit_bytes=16 << 20),
    )(*(pltpu.with_memory_space_constraint(a, pltpu.HBM) for a in (state, velocity, weights)), proj, diff, table, land, land)


def remap(recv, land, import_proj, weights, arrived, tracer):
    chunk = 16
    return pl.pallas_call(
        functools.partial(remap_kernel, chunk),
        name="remap",
        out_shape=(
            jax.ShapeDtypeStruct((LEV, ROWS, TILE), F32),
            jax.ShapeDtypeStruct((ROWS, FLD, TILE), BF16),
        ),
        in_specs=[SMEM, SMEM, SMEM, VMEM, VMEM, VMEM],
        out_specs=(ANY, ANY),
        scratch_shapes=[
            pltpu.VMEM((LEV, ROWS, TILE), F32),
            pltpu.VMEM((ROWS, FLD, TILE), BF16),
            pltpu.VMEM((FLD, LEV, TILE), F32),
            pltpu.SemaphoreType.DMA((2, ROWS // chunk)),
        ],
        compiler_params=pltpu.CompilerParams(vmem_limit_bytes=16 << 20),
    )(recv, land, import_proj, *(pltpu.with_memory_space_constraint(a, pltpu.VMEM) for a in (weights, arrived, tracer)))


def per_device(
    state, velocity, diffusivity, export_proj, import_proj, intersection_weights, recv_slots, send_slots, land
):
    land = land.reshape(1, ROWS)
    table = send_slots[:, 0, 0].transpose(0, 2, 1)
    recv = recv_slots[0, :, 0].T
    arrived, tracer, weights = exchange(
        state[0], velocity[0], intersection_weights[0, :, 0], export_proj[0], diffusivity, table, land
    )
    new_state, imported = remap(recv, land, import_proj[0].T, weights, arrived, tracer)
    return new_state[None], imported[None]


def solution(mesh):
    return jax.shard_map(
        per_device,
        mesh=mesh,
        in_specs=(
            P("comp", None, "gx", "gy"),
            P("comp", None, None, "gx", "gy"),
            P("comp", None),
            P("comp", None, None),
            P("comp", None, None),
            P("comp", "gx", "gy", None, None, None),
            P("comp", "gx", "gy", None),
            P(None, "gx", "gy", None, None),
            P("gx", "gy"),
        ),
        out_specs=(P("comp", None, "gx", "gy"), P("comp", "gx", None, "gy")),
        check_vma=False,
    )
```

time: 129 us -> 61.3 us (0.48)
  the two profiles are of different devices: /device:TPU:30 before, /device:TPU:13 now
where the time goes in v1:
time: 61.3 us; the launch traced here: 61.1 us
  Pallas kernels  57.7 us (94%)
  local copies, waits for them, and re-layouts  2.73 us (4%)
  between operations  0.68 us (1%)
    pallas_call x1, Pallas kernels, exchange(): pl.pallas_call(exchange_kernel, name='exchange', out_shape=(pltpu.VMEM((G...  50.3 us
    pallas_call x1, Pallas kernels, remap(): pl.pallas_call(functools.partial(remap_kernel, chunk), name='remap', out_...  7.36 us
    unnamed x12, local copies, waits for them, and re-layouts  2.73 us

profile of v1, /device:TPU:13, one launch (start us, length us, event | category | flops | bytes accessed | tf_op | source)
XLA Modules:
  0.0 61.1 jit_solution(16021161102404119724)
XLA Ops:
  0.6 0.0 copy-start.4
  0.6 0.0 copy-start.2
  0.7 0.0 copy-start
  0.7 0.7 %copy-done = s32[2,1,1,64,16]{3,4,2,1,0:T(8,128)S(1)} copy-done((s32[2,1,1,64,16]{3,4,2,1,0:T(8,128)S(1)}, s32[2,1,1,64,16]{3,4,2,1,0:T(8,128)}, u32[]{:S(2)}) %copy-start) | copy-done | bytes 8216
  1.4 0.0 copy-start.1
  1.4 0.7 %copy-done.1 = s32[128,1]{0,1:T(1,128)S(1)} copy-done((s32[128,1]{0,1:T(1,128)S(1)}, s32[128,1]{0,1:T(1,128)}, u32[]{:S(2)}) %copy-start.1) | copy-done | bytes 536
  2.0 0.0 copy-start.3
  2.0 0.7 %copy-done.3 = f32[1,8,16]{2,1,0:T(8,128)S(1)} copy-done((f32[1,8,16]{2,1,0:T(8,128)S(1)}, f32[1,8,16]{2,1,0:T(8,128)}, u32[]{:S(2)}) %copy-start.3) | copy-done | bytes 536
  2.7 0.0 copy-start.5
  2.7 0.7 %copy-done.5 = f32[1,16]{1,0:T(1,128)S(1)} copy-done((f32[1,16]{1,0:T(1,128)S(1)}, f32[1,16]{1,0:T(1,128)}, u32[]{:S(2)}) %copy-start.5) | copy-done | bytes 88
  3.4 50.3 %exchange.1 = (bf16[1024,8,128]{2,1,0:T(8,128)(2,1)S(1)}, f32[16,128,128]{2,1,0:T(8,128)S(1)}, bf16[128,4,128,128]{3,2,1,0:T(8,128)(2,1)S(1)}) custom-call(f32[16,128,128]{2,1,0:T(8,128)} %bitcast.24, bf16[2,16,128,128]{3,2,1,0:T(8,128)(2,1)} %bitcast.25, bf16[128,4,128,128]{3,2,1,0:T(8,128)(2,1)} %bitcast.23, f32[8,16]{1,0:T(8,128)S(1)} %bitcast.21, ...), custom_call_target="tpu_custom_call" | custom-call | tf_op jit(solution)/shard_map/exchange/pallas_call | solution.py:244
  53.7 0.0 copy-done.4
  53.7 0.0 copy-done.2
  53.7 7.4 %remap.1 = (f32[16,128,128]{2,1,0:T(8,128)}, bf16[128,8,128]{2,1,0:T(8,128)(2,1)}) custom-call(s32[4,128]{1,0:T(4,128)S(1)} %bitcast.22, s32[1,128]{1,0:T(1,128)S(1)} %bitcast.19, f32[8,16]{1,0:T(8,128)S(1)} %bitcast.20, bf16[128,4,128,128]{3,2,1,0:T(8,128)(2,1)S(1)} %get-tuple-element.7.w, bf16[1024,8,128]{2,1,0:T(8,128)(2,1)S(1)} %get-tuple-element.8.arrived, ...), custom_call_target="tpu_custom_call" | custom-call | tf_op jit(solution)/shard_map/remap/pallas_call | solution.py:277
Async XLA Ops:
  0.6 53.1 %copy-start.4 = (s32[1,128,1,4]{1,3,2,0:T(4,128)S(1)}, s32[1,128,1,4]{1,3,2,0:T(4,128)}, u32[]{:S(2)}) copy-start(s32[1,128,1,4]{1,3,2,0:T(4,128)} %param.15) | copy-start | bytes 6148
  0.6 53.1 %copy-start.2 = (f32[1,16,8]{1,2,0:T(8,128)S(1)}, f32[1,16,8]{1,2,0:T(8,128)}, u32[]{:S(2)}) copy-start(f32[1,16,8]{1,2,0:T(8,128)} %param.13) | copy-start | bytes 1540
  0.7 0.7 %copy-start = (s32[2,1,1,64,16]{3,4,2,1,0:T(8,128)S(1)}, s32[2,1,1,64,16]{3,4,2,1,0:T(8,128)}, u32[]{:S(2)}) copy-start(s32[2,1,1,64,16]{3,4,2,1,0:T(8,128)} %param.16) | copy-start | bytes 24580
  1.4 0.7 %copy-start.1 = (s32[128,1]{0,1:T(1,128)S(1)}, s32[128,1]{0,1:T(1,128)}, u32[]{:S(2)}) copy-start(s32[128,1]{0,1:T(1,128)} %param.17) | copy-start | bytes 1540
  2.0 0.7 %copy-start.3 = (f32[1,8,16]{2,1,0:T(8,128)S(1)}, f32[1,8,16]{2,1,0:T(8,128)}, u32[]{:S(2)}) copy-start(f32[1,8,16]{2,1,0:T(8,128)} %param.12) | copy-start | bytes 1540
  2.7 0.7 %copy-start.5 = (f32[1,16]{1,0:T(1,128)S(1)}, f32[1,16]{1,0:T(1,128)}, u32[]{:S(2)}) copy-start(f32[1,16]{1,0:T(1,128)} %diff.1) | copy-start | bytes 196

commit v2 on v1

--- a/solution.py
+++ b/solution.py
@@ -18,22 +18,27 @@
 TOP = 8
 PADDED = ROWS + 2 * TOP
 W_PARTS = 8
-FIRST, SECOND = 12, 44
+FIRST, SECOND = 16, 48
 
 
 def partner(turn, gx, gy):
-    x = lax.rem(lax.div(gx, 2) + lax.div(turn, 16), 4)
-    core = lax.rem(lax.rem(gx, 2) + lax.rem(lax.div(turn, 8), 2), 2)
-    y = lax.rem(lax.div(gy, 2) + lax.rem(lax.div(turn, 2), 4), 4)
-    high = lax.rem(lax.rem(gy, 2) + lax.rem(turn, 2), 2)
+    block, i = lax.div(turn, 16), lax.rem(turn, 16)
+    step_x = lax.rem(i, 4)
+    step_y = lax.rem(lax.div(i, 4) + i, 4)
+    step_high = lax.rem(i + block, 2)
+    step_core = lax.div(block, 2)
+    x = lax.rem(lax.div(gx, 2) + step_x, 4)
+    core = lax.rem(gx + step_core, 2)
+    y = lax.rem(lax.div(gy, 2) + step_y, 4)
+    high = lax.rem(gy + step_high, 2)
     return x * 2 + core, y * 2 + high
 
 
 def exchange_kernel(
-    state_hbm, vel_hbm, w_hbm, proj, diff, table, land, land_row,
-    arrived, tracer, w_out,
-    ta, tb, vel, ex, buf, halo_out, halo_in, wet,
-    sem_state, sem_vel, sem_w, sem_send, sem_recv, sem_hs, sem_hr,
+    state_hbm, vel_hbm, w_hbm, proj_hbm, diff_hbm, table_hbm, land_hbm, recv_hbm, ip_hbm,
+    arrived, tracer, w_out, spread, recv_out, land_out,
+    ta, tb, vel, ex, buf, halo_out, halo_in, edge, wet, proj, land_row, diff, table, ip,
+    sem_state, sem_vel, sem_small, sem_w, sem_send, sem_recv, sem_hs, sem_hr,
 ):
     comp, gx, gy = lax.axis_index("comp"), lax.axis_index("gx"), lax.axis_index("gy")
     other = 1 - comp
@@ -42,9 +47,27 @@
     left, right = lax.rem(gy + N_GY - 1, N_GY), lax.rem(gy + 1, N_GY)
     beside = ((comp, up, gy), (comp, down, gy), (comp, gx, left), (comp, gx, right))
 
+    small = [
+        pltpu.make_async_copy(source, target, sem_small.at[i])
+        for i, (source, target) in enumerate(
+            (
+                (proj_hbm, proj),
+                (land_hbm, land_row),
+                (land_hbm, land_out),
+                (table_hbm, table),
+                (diff_hbm, diff),
+                (recv_hbm, recv_out),
+                (ip_hbm, ip),
+            )
+        )
+    ]
     interior = pl.ds(TOP, ROWS)
+    for copy in small[:3]:
+        copy.start()
     get_state = pltpu.make_async_copy(state_hbm, ta.at[:, interior], sem_state)
     get_state.start()
+    for copy in small[3:]:
+        copy.start()
     get_vel = pltpu.make_async_copy(vel_hbm, vel, sem_vel)
     get_vel.start()
 
@@ -68,6 +91,9 @@
 
     for i in range(W_PARTS):
         get_w(i).start()
+
+    for copy in small:
+        copy.wait()
 
     row_wet = jnp.where(comp == 0, jnp.ones((1, TILE), F32), land_row[...].astype(F32))
     wet[...] = jnp.transpose(jnp.broadcast_to(row_wet, (ROWS, TILE)))
@@ -81,7 +107,7 @@
             total = columns[0] * ta[0, pl.ds(TOP + x, 1), :]
             for l in range(1, LEV):
                 total += columns[l] * ta[l, pl.ds(TOP + x, 1), :]
-            ex[x] = total * jnp.where(comp == 0, 1.0, land[0, x].astype(F32))
+            ex[x] = total * jnp.where(comp == 0, 1.0, land_out[0, x].astype(F32))
         return carry
 
     lax.fori_loop(0, ROWS // 4, export, 0)
@@ -108,6 +134,10 @@
         hit = ((r == l) & (c == 0)) | ((r == LEV + l) & (c == TILE - 1))
         return jnp.where(hit, 1.0, 0.0).astype(BF16)
 
+    r = lax.broadcasted_iota(jnp.int32, (FLD, TILE), 0)
+    c = lax.broadcasted_iota(jnp.int32, (FLD, TILE), 1)
+    both_ends = jnp.where(((r == 0) & (c == 0)) | ((r == 1) & (c == TILE - 1)), 1.0, 0.0).astype(BF16)
+
     def halo_copy(turn, side):
         return pltpu.make_async_remote_copy(
             src_ref=halo_out.at[turn, side],
@@ -123,14 +153,14 @@
         halo_out[turn, 0] = flat[pl.ds(TOP, LEV, stride=PADDED), :].astype(BF16)
         halo_out[turn, 1] = flat[pl.ds(TOP + ROWS - 1, LEV, stride=PADDED), :].astype(BF16)
 
-        def add(l, total):
-            return total + lax.dot_general(
-                pick(l), t[l, interior, :].astype(BF16), (((1,), (1,)), ((), ())), preferred_element_type=F32
+        for l in range(LEV):
+            ends = lax.dot_general(
+                both_ends, t[l, interior, :].astype(BF16), (((1,), (1,)), ((), ())), preferred_element_type=F32
             )
-
-        edges = lax.fori_loop(0, LEV, add, jnp.zeros((2 * LEV, TILE), F32)).astype(BF16)
-        halo_out[turn, 2] = edges[:LEV]
-        halo_out[turn, 3] = edges[LEV:]
+            edge[0, l : l + 1, :] = ends[0:1]
+            edge[1, l : l + 1, :] = ends[1:2]
+        halo_out[turn, 2] = edge[0].astype(BF16)
+        halo_out[turn, 3] = edge[1].astype(BF16)
         for side in range(4):
             halo_copy(turn, side).start()
 
@@ -180,6 +210,9 @@
     edges = take_halo(1, tb)
     advance(tb, edges, put_tracer)
 
+    for f in range(FLD):
+        for l in range(LEV):
+            spread[f, l : l + 1, :] = jnp.full((1, TILE), ip[f, l], F32)
     for i in range(W_PARTS):
         get_w(i).wait()
     for turn in range(2):
@@ -189,7 +222,7 @@
     pltpu.make_async_copy(arrived, arrived, sem_recv).wait()
 
 
-def remap_kernel(chunk, recv, land, ip, w, arrived, tracer, new_hbm, imp_hbm, new, imp, spread, sem_out):
+def remap_kernel(chunk, recv, land, w, arrived, tracer, spread, new_hbm, imp_hbm, new, imp, sem_out):
     comp = lax.axis_index("comp")
 
     def out_copies(i):
@@ -199,9 +232,6 @@
             pltpu.make_async_copy(imp.at[rows], imp_hbm.at[rows], sem_out.at[1, i]),
         )
 
-    for f in range(FLD):
-        for l in range(LEV):
-            spread[f, l : l + 1, :] = jnp.full((1, TILE), ip[f, l], F32)
     tracer_rows = tracer.reshape(LEV * ROWS, TILE)
     new_rows = new.reshape(LEV * ROWS, TILE)
 
@@ -239,7 +269,11 @@
 SMEM = pl.BlockSpec(memory_space=pltpu.SMEM)
 
 
-def exchange(state, velocity, weights, proj, diff, table, land):
+def kept_in(space, arrays):
+    return [pltpu.with_memory_space_constraint(a, space) for a in arrays]
+
+
+def exchange(*arrays):
     dma = pltpu.SemaphoreType.DMA
     return pl.pallas_call(
         exchange_kernel,
@@ -248,9 +282,12 @@
             pltpu.VMEM((GROUP * CAP, FLD, TILE), BF16),
             pltpu.VMEM((LEV, ROWS, TILE), F32),
             pltpu.VMEM((ROWS, K, TILE, TILE), BF16),
+            pltpu.VMEM((FLD, LEV, TILE), F32),
+            pltpu.SMEM((K, ROWS), jnp.int32),
+            pltpu.SMEM((1, ROWS), jnp.int32),
         ),
-        in_specs=[HBM, HBM, HBM, VMEM, SMEM, SMEM, SMEM, VMEM],
-        out_specs=(VMEM, VMEM, VMEM),
+        in_specs=[HBM] * 9,
+        out_specs=(VMEM, VMEM, VMEM, VMEM, SMEM, SMEM),
         scratch_shapes=[
             pltpu.VMEM((LEV, PADDED, TILE), F32),
             pltpu.VMEM((LEV, PADDED, TILE), F32),
@@ -259,9 +296,16 @@
             pltpu.VMEM((GROUP * CAP, FLD, TILE), BF16),
             pltpu.VMEM((2, 4, LEV, TILE), BF16),
             pltpu.VMEM((2, 4, LEV, TILE), BF16),
+            pltpu.VMEM((2, LEV, TILE), F32),
             pltpu.VMEM((ROWS, TILE), F32),
+            pltpu.VMEM((FLD, LEV), F32),
+            pltpu.VMEM((1, ROWS), jnp.int32),
+            pltpu.SMEM((1, LEV), F32),
+            pltpu.SMEM((2, CAP, GROUP), jnp.int32),
+            pltpu.SMEM((FLD, LEV), F32),
             dma,
             dma,
+            dma((7,)),
             dma((W_PARTS,)),
             dma,
             dma,
@@ -269,11 +313,11 @@
             dma((2, 4)),
         ],
         compiler_params=pltpu.CompilerParams(collective_id=0, has_side_effects=True, vmem_limit_bytes=16 << 20),
-    )(*(pltpu.with_memory_space_constraint(a, pltpu.HBM) for a in (state, velocity, weights)), proj, diff, table, land, land)
-
-
-def remap(recv, land, import_proj, weights, arrived, tracer):
-    chunk = 16
+    )(*kept_in(pltpu.HBM, arrays))
+
+
+def remap(recv, land, weights, arrived, tracer, spread):
+    chunk = 32
     return pl.pallas_call(
         functools.partial(remap_kernel, chunk),
         name="remap",
@@ -281,16 +325,15 @@
             jax.ShapeDtypeStruct((LEV, ROWS, TILE), F32),
             jax.ShapeDtypeStruct((ROWS, FLD, TILE), BF16),
         ),
-        in_specs=[SMEM, SMEM, SMEM, VMEM, VMEM, VMEM],
+        in_specs=[SMEM, SMEM, VMEM, VMEM, VMEM, VMEM],
         out_specs=(ANY, ANY),
         scratch_shapes=[
             pltpu.VMEM((LEV, ROWS, TILE), F32),
             pltpu.VMEM((ROWS, FLD, TILE), BF16),
-            pltpu.VMEM((FLD, LEV, TILE), F32),
             pltpu.SemaphoreType.DMA((2, ROWS // chunk)),
         ],
         compiler_params=pltpu.CompilerParams(vmem_limit_bytes=16 << 20),
-    )(recv, land, import_proj, *(pltpu.with_memory_space_constraint(a, pltpu.VMEM) for a in (weights, arrived, tracer)))
+    )(*kept_in(pltpu.SMEM, (recv, land)), *kept_in(pltpu.VMEM, (weights, arrived, tracer, spread)))
 
 
 def per_device(
@@ -299,10 +342,11 @@
     land = land.reshape(1, ROWS)
     table = send_slots[:, 0, 0].transpose(0, 2, 1)
     recv = recv_slots[0, :, 0].T
-    arrived, tracer, weights = exchange(
-        state[0], velocity[0], intersection_weights[0, :, 0], export_proj[0], diffusivity, table, land
+    arrived, tracer, weights, spread, recv, land = exchange(
+        state[0], velocity[0], intersection_weights[0, :, 0], export_proj[0], diffusivity, table, land, recv,
+        import_proj[0].T,
     )
-    new_state, imported = remap(recv, land, import_proj[0].T, weights, arrived, tracer)
+    new_state, imported = remap(recv, land, weights, arrived, tracer, spread)
     return new_state[None], imported[None]
 
 

time: 61.3 us -> 43.4 us (0.71)
  the two profiles are of different devices: /device:TPU:13 before, /device:TPU:1 now
where the time goes in v2:
time: 43.4 us; the launch traced here: 43.1 us
  Pallas kernels  42.5 us (98%)
  between operations  0.64 us (1%)
    pallas_call x1, Pallas kernels, exchange(): pl.pallas_call(exchange_kernel, name='exchange', out_shape=(pltpu.VMEM((G...  36.4 us
    pallas_call x1, Pallas kernels, remap(): pl.pallas_call(functools.partial(remap_kernel, chunk), name='remap', out_...  6.07 us

profile of v2, /device:TPU:1, one launch (start us, length us, event | category | flops | bytes accessed | tf_op | source)
XLA Modules:
  0.0 43.1 jit_solution(6633589016602917286)
XLA Ops:
  0.6 36.4 %exchange.1 = (bf16[1024,8,128]{2,1,0:T(8,128)(2,1)S(1)}, f32[16,128,128]{2,1,0:T(8,128)S(1)}, bf16[128,4,128,128]{3,2,1,0:T(8,128)(2,1)S(1)}, f32[8,16,128]{2,1...) custom-call(f32[16,128,128]{2,1,0:T(8,128)} %bitcast.17, bf16[2,16,128,128]{3,2,1,0:T(8,128)(2,1)} %bitcast.18, ...), custom_call_target="tpu_custom_call" | custom-call | tf_op jit(solution)/shard_map/exchange/pallas_call | solution.py:278
  37.1 6.1 %remap.1 = (f32[16,128,128]{2,1,0:T(8,128)}, bf16[128,8,128]{2,1,0:T(8,128)(2,1)}) custom-call(s32[4,128]{1,0:T(4,128)S(4)} %get-tuple-element.10.recv, s32[1,128]{1,0:T(1,128)S(4)} %get-tuple-element.11.land, bf16[128,4,128,128]{3,2,1,0:T(8,128)(2,1)S(1)} %get-tuple-element.12.w, bf16[1024,8,128]{2,1,0:T(8,128)(2,1)S(1)} %get-tuple-element.13.arrived, ...), custom_call_target="tpu_custom_call" | custom-call | tf_op jit(solution)/shard_map/remap/pallas_call | solution.py:321

commit v3 on v2

--- a/solution.py
+++ b/solution.py
@@ -18,6 +18,7 @@
 TOP = 8
 PADDED = ROWS + 2 * TOP
 W_PARTS = 8
+TURNED = 4
 FIRST, SECOND = 16, 48
 
 
@@ -207,14 +208,22 @@
     advance(ta, edges, put_tb)
     send_halo(1, tb)
     lax.fori_loop(SECOND, GROUP, serve, 0)
+
+    def turn_w(i, carry):
+        for j in range(TURNED):
+            for k in range(K):
+                w_out[i * TURNED + j, k] = jnp.transpose(w_out[i * TURNED + j, k])
+        return carry
+
+    for i in range(W_PARTS):
+        get_w(i).wait()
+    lax.fori_loop(0, ROWS // TURNED, turn_w, 0)
     edges = take_halo(1, tb)
     advance(tb, edges, put_tracer)
 
     for f in range(FLD):
         for l in range(LEV):
             spread[f, l : l + 1, :] = jnp.full((1, TILE), ip[f, l], F32)
-    for i in range(W_PARTS):
-        get_w(i).wait()
     for turn in range(2):
         for side in range(4):
             halo_copy(turn, side).wait_send()
@@ -240,8 +249,8 @@
             x = i * chunk + j
             wet = jnp.where(comp == 0, 1.0, land[0, x].astype(F32))
             source = jnp.concatenate([arrived[recv[k, x]] for k in range(K)], axis=1)
-            weights = jnp.concatenate([w[x, k] for k in range(K)], axis=1)
-            summed = lax.dot_general(source, weights, (((1,), (1,)), ((), ())), preferred_element_type=F32)
+            weights = jnp.concatenate([w[x, k] for k in range(K)], axis=0)
+            summed = jnp.dot(source, weights, preferred_element_type=F32)
             got = (summed * wet).astype(BF16)
             imp[x] = got
             got = got.astype(F32)

time: 43.4 us -> 41.6 us (0.959)
  Pallas kernels: 42.5 us -> 40.7 us
    pallas_call x1, Pallas kernels: 6.07 us -> 4.28 us  [remap(): pl.pallas_call(functools.partial(remap_kernel, chunk), name='remap', out_...]
where the time goes in v3:
time: 41.6 us; the launch traced here: 41.3 us
  Pallas kernels  40.7 us (98%)
  between operations  0.64 us (2%)
    pallas_call x1, Pallas kernels, exchange(): pl.pallas_call(exchange_kernel, name='exchange', out_shape=(pltpu.VMEM((G...  36.4 us
    pallas_call x1, Pallas kernels, remap(): pl.pallas_call(functools.partial(remap_kernel, chunk), name='remap', out_...  4.28 us

profile of v3, /device:TPU:1, one launch (start us, length us, event | category | flops | bytes accessed | tf_op | source)
XLA Modules:
  0.0 41.3 jit_solution(1799181741415987083)
XLA Ops:
  0.6 36.4 %exchange.1 = (bf16[1024,8,128]{2,1,0:T(8,128)(2,1)S(1)}, f32[16,128,128]{2,1,0:T(8,128)S(1)}, bf16[128,4,128,128]{3,2,1,0:T(8,128)(2,1)S(1)}, f32[8,16,128]{2,1...) custom-call(f32[16,128,128]{2,1,0:T(8,128)} %bitcast.17, bf16[2,16,128,128]{3,2,1,0:T(8,128)(2,1)} %bitcast.18, ...), custom_call_target="tpu_custom_call" | custom-call | tf_op jit(solution)/shard_map/exchange/pallas_call | solution.py:287
  37.1 4.3 %remap.1 = (f32[16,128,128]{2,1,0:T(8,128)}, bf16[128,8,128]{2,1,0:T(8,128)(2,1)}) custom-call(s32[4,128]{1,0:T(4,128)S(4)} %get-tuple-element.10.recv, s32[1,128]{1,0:T(1,128)S(4)} %get-tuple-element.11.land, bf16[128,4,128,128]{3,2,1,0:T(8,128)(2,1)S(1)} %get-tuple-element.12.w, bf16[1024,8,128]{2,1,0:T(8,128)(2,1)S(1)} %get-tuple-element.13.arrived, ...), custom_call_target="tpu_custom_call" | custom-call | tf_op jit(solution)/shard_map/remap/pallas_call | solution.py:330

commit v4 on v3

--- a/solution.py
+++ b/solution.py
@@ -1,5 +1,3 @@
-import functools
-
 import jax
 import jax.numpy as jnp
 from jax import lax
@@ -18,8 +16,10 @@
 TOP = 8
 PADDED = ROWS + 2 * TOP
 W_PARTS = 8
+S_PARTS = 4
+OUT_ROWS = 8
 TURNED = 4
-FIRST, SECOND = 16, 48
+FIRST, SECOND = 4, 36
 
 
 def partner(turn, gx, gy):
@@ -53,9 +53,9 @@
         for i, (source, target) in enumerate(
             (
                 (proj_hbm, proj),
-                (land_hbm, land_row),
                 (land_hbm, land_out),
                 (table_hbm, table),
+                (land_hbm, land_row),
                 (diff_hbm, diff),
                 (recv_hbm, recv_out),
                 (ip_hbm, ip),
@@ -63,27 +63,25 @@
         )
     ]
     interior = pl.ds(TOP, ROWS)
-    for copy in small[:3]:
-        copy.start()
-    get_state = pltpu.make_async_copy(state_hbm, ta.at[:, interior], sem_state)
-    get_state.start()
-    for copy in small[3:]:
+    slab = ROWS // S_PARTS
+
+    def get_state(i):
+        return pltpu.make_async_copy(
+            state_hbm.at[:, pl.ds(i * slab, slab)], ta.at[:, pl.ds(TOP + i * slab, slab)], sem_state.at[i]
+        )
+
+    for i in range(S_PARTS):
+        get_state(i).start()
+    barrier = pltpu.get_barrier_semaphore()
+    for d in range(GROUP):
+        pl.semaphore_signal(barrier, inc=1, device_id=(other, d // N_GY, d % N_GY), device_id_type=MESH)
+    for device in beside:
+        pl.semaphore_signal(barrier, inc=1, device_id=device, device_id_type=MESH)
+    for copy in small:
         copy.start()
     get_vel = pltpu.make_async_copy(vel_hbm, vel, sem_vel)
     get_vel.start()
 
-    barrier = pltpu.get_barrier_semaphore()
-    for device in beside:
-        pl.semaphore_signal(barrier, inc=1, device_id=device, device_id_type=MESH)
-
-    def greet(d, carry):
-        pl.semaphore_signal(
-            barrier, inc=1, device_id=(other, lax.div(d, N_GY), lax.rem(d, N_GY)), device_id_type=MESH
-        )
-        return carry
-
-    lax.fori_loop(0, GROUP, greet, 0)
-
     part = w_hbm.shape[0] // W_PARTS
 
     def get_w(i):
@@ -93,25 +91,22 @@
     for i in range(W_PARTS):
         get_w(i).start()
 
-    for copy in small:
+    for copy in small[:3]:
         copy.wait()
-
-    row_wet = jnp.where(comp == 0, jnp.ones((1, TILE), F32), land_row[...].astype(F32))
-    wet[...] = jnp.transpose(jnp.broadcast_to(row_wet, (ROWS, TILE)))
-
     columns = [jnp.broadcast_to(proj[:, l : l + 1], (FLD, TILE)) for l in range(LEV)]
-    get_state.wait()
 
     def export(i, carry):
-        for j in range(4):
-            x = i * 4 + j
+        for j in range(8):
+            x = i * 8 + j
             total = columns[0] * ta[0, pl.ds(TOP + x, 1), :]
             for l in range(1, LEV):
                 total += columns[l] * ta[l, pl.ds(TOP + x, 1), :]
             ex[x] = total * jnp.where(comp == 0, 1.0, land_out[0, x].astype(F32))
         return carry
 
-    lax.fori_loop(0, ROWS // 4, export, 0)
+    for i in range(S_PARTS):
+        get_state(i).wait()
+        lax.fori_loop(i * slab // 8, (i + 1) * slab // 8, export, 0)
     pl.semaphore_wait(barrier, GROUP + 4)
 
     def serve(turn, carry):
@@ -201,6 +196,10 @@
         tracer[l] = value
 
     lax.fori_loop(0, FIRST, serve, 0)
+    for copy in small[3:]:
+        copy.wait()
+    row_wet = jnp.where(comp == 0, jnp.ones((1, TILE), F32), land_row[...].astype(F32))
+    wet[...] = jnp.transpose(jnp.broadcast_to(row_wet, (ROWS, TILE)))
     send_halo(0, ta)
     lax.fori_loop(FIRST, SECOND, serve, 0)
     edges = take_halo(0, ta)
@@ -231,45 +230,32 @@
     pltpu.make_async_copy(arrived, arrived, sem_recv).wait()
 
 
-def remap_kernel(chunk, recv, land, w, arrived, tracer, spread, new_hbm, imp_hbm, new, imp, sem_out):
+def remap_kernel(recv, land, w, arrived, tracer, spread, new_hbm, imp_hbm, new, imp, sem_out):
     comp = lax.axis_index("comp")
-
-    def out_copies(i):
-        rows = pl.ds(pl.multiple_of(i * chunk, chunk), chunk)
-        return (
-            pltpu.make_async_copy(new.at[:, rows], new_hbm.at[:, rows], sem_out.at[0, i]),
-            pltpu.make_async_copy(imp.at[rows], imp_hbm.at[rows], sem_out.at[1, i]),
-        )
-
     tracer_rows = tracer.reshape(LEV * ROWS, TILE)
     new_rows = new.reshape(LEV * ROWS, TILE)
-
-    def step(i, carry):
-        for j in range(chunk):
-            x = i * chunk + j
-            wet = jnp.where(comp == 0, 1.0, land[0, x].astype(F32))
-            source = jnp.concatenate([arrived[recv[k, x]] for k in range(K)], axis=1)
-            weights = jnp.concatenate([w[x, k] for k in range(K)], axis=0)
-            summed = jnp.dot(source, weights, preferred_element_type=F32)
-            got = (summed * wet).astype(BF16)
-            imp[x] = got
-            got = got.astype(F32)
-            force = spread[0] * got[0:1, :]
-            for f in range(1, FLD):
-                force += spread[f] * got[f : f + 1, :]
-            rows = pl.ds(x, LEV, stride=ROWS)
-            new_rows[rows, :] = tracer_rows[rows, :] + wet * force
-        for copy in out_copies(i):
-            copy.start()
-        return carry
-
-    def drain(i, carry):
-        for copy in out_copies(i):
-            copy.wait()
-        return carry
-
-    lax.fori_loop(0, ROWS // chunk, step, 0)
-    lax.fori_loop(0, ROWS // chunk, drain, 0)
+    copies = []
+    for x in range(ROWS):
+        wet = jnp.where(comp == 0, 1.0, land[0, x].astype(F32))
+        source = jnp.concatenate([arrived[recv[k, x]] for k in range(K)], axis=1)
+        weights = jnp.concatenate([w[x, k] for k in range(K)], axis=0)
+        got = (jnp.dot(source, weights, preferred_element_type=F32) * wet).astype(BF16)
+        imp[x] = got
+        got = got.astype(F32)
+        force = spread[0] * got[0:1, :]
+        for f in range(1, FLD):
+            force += spread[f] * got[f : f + 1, :]
+        rows = pl.ds(x, LEV, stride=ROWS)
+        new_rows[rows, :] = tracer_rows[rows, :] + wet * force
+        if x % OUT_ROWS == OUT_ROWS - 1:
+            i = x // OUT_ROWS
+            done = pl.ds(i * OUT_ROWS, OUT_ROWS)
+            copies.append(pltpu.make_async_copy(new.at[:, done], new_hbm.at[:, done], sem_out.at[0, i]))
+            copies.append(pltpu.make_async_copy(imp.at[done], imp_hbm.at[done], sem_out.at[1, i]))
+            copies[-2].start()
+            copies[-1].start()
+    for copy in copies:
+        copy.wait()
 
 
 ANY = pl.BlockSpec(memory_space=pl.ANY)
@@ -312,7 +298,7 @@
             pltpu.SMEM((1, LEV), F32),
             pltpu.SMEM((2, CAP, GROUP), jnp.int32),
             pltpu.SMEM((FLD, LEV), F32),
-            dma,
+            dma((S_PARTS,)),
             dma,
             dma((7,)),
             dma((W_PARTS,)),
@@ -326,9 +312,8 @@
 
 
 def remap(recv, land, weights, arrived, tracer, spread):
-    chunk = 32
     return pl.pallas_call(
-        functools.partial(remap_kernel, chunk),
+        remap_kernel,
         name="remap",
         out_shape=(
             jax.ShapeDtypeStruct((LEV, ROWS, TILE), F32),
@@ -339,7 +324,7 @@
         scratch_shapes=[
             pltpu.VMEM((LEV, ROWS, TILE), F32),
             pltpu.VMEM((ROWS, FLD, TILE), BF16),
-            pltpu.SemaphoreType.DMA((2, ROWS // chunk)),
+            pltpu.SemaphoreType.DMA((2, ROWS // OUT_ROWS)),
         ],
         compiler_params=pltpu.CompilerParams(vmem_limit_bytes=16 << 20),
     )(*kept_in(pltpu.SMEM, (recv, land)), *kept_in(pltpu.VMEM, (weights, arrived, tracer, spread)))

time: 41.6 us -> 41.2 us (level)
  no operation moved by 1% of the time
where the time goes in v4:
time: 41.2 us; the launch traced here: 41.1 us
  Pallas kernels  40.5 us (98%)
  between operations  0.64 us (2%)
    pallas_call x1, Pallas kernels, exchange(): pl.pallas_call(exchange_kernel, name='exchange', out_shape=(pltpu.VMEM((G...  36.5 us
    pallas_call x1, Pallas kernels, remap(): pl.pallas_call(remap_kernel, name='remap', out_shape=(jax.ShapeDtypeStruc...  4.02 us

profile of v4, /device:TPU:1, one launch (start us, length us, event | category | flops | bytes accessed | tf_op | source)
XLA Modules:
  0.0 41.1 jit_solution(5683280791734642650)
XLA Ops:
  0.6 36.5 %exchange.1 = (bf16[1024,8,128]{2,1,0:T(8,128)(2,1)S(1)}, f32[16,128,128]{2,1,0:T(8,128)S(1)}, bf16[128,4,128,128]{3,2,1,0:T(8,128)(2,1)S(1)}, f32[8,16,128]{2,1...) custom-call(f32[16,128,128]{2,1,0:T(8,128)} %bitcast.17, bf16[2,16,128,128]{3,2,1,0:T(8,128)(2,1)} %bitcast.18, ...), custom_call_target="tpu_custom_call" | custom-call | tf_op jit(solution)/shard_map/exchange/pallas_call | solution.py:273
  37.1 4.0 %remap.1 = (f32[16,128,128]{2,1,0:T(8,128)}, bf16[128,8,128]{2,1,0:T(8,128)(2,1)}) custom-call(s32[4,128]{1,0:T(4,128)S(4)} %get-tuple-element.10.recv, s32[1,128]{1,0:T(1,128)S(4)} %get-tuple-element.11.land, bf16[128,4,128,128]{3,2,1,0:T(8,128)(2,1)S(1)} %get-tuple-element.12.w, bf16[1024,8,128]{2,1,0:T(8,128)(2,1)S(1)} %get-tuple-element.13.arrived, ...), custom_call_target="tpu_custom_call" | custom-call | tf_op jit(solution)/shard_map/remap/pallas_call | solution.py:315

commit v5 on v4

--- a/solution.py
+++ b/solution.py
@@ -19,27 +19,26 @@
 S_PARTS = 4
 OUT_ROWS = 8
 TURNED = 4
-FIRST, SECOND = 4, 36
-
-
-def partner(turn, gx, gy):
-    block, i = lax.div(turn, 16), lax.rem(turn, 16)
-    step_x = lax.rem(i, 4)
-    step_y = lax.rem(lax.div(i, 4) + i, 4)
-    step_high = lax.rem(i + block, 2)
-    step_core = lax.div(block, 2)
-    x = lax.rem(lax.div(gx, 2) + step_x, 4)
-    core = lax.rem(gx + step_core, 2)
-    y = lax.rem(lax.div(gy, 2) + step_y, 4)
-    high = lax.rem(gy + step_high, 2)
-    return x * 2 + core, y * 2 + high
+SELF = 2 * CAP
+EACH = tuple((core, high) for core in range(2) for high in range(2))
+STRAIGHT = ((1, 1), (3, 3))
+VIA_Z = ((0, 1), (1, 0), (0, 3), (3, 0), (1, 3), (3, 1), (0, 0))
+NEAR = (0, 1, 3)
+
+
+def place(gx, gy, dx, core, dy, high):
+    to_x = lax.rem(lax.div(gx, 2) + dx, 4) * 2 + lax.rem(gx + core, 2)
+    to_y = lax.rem(lax.div(gy, 2) + dy, 4) * 2 + lax.rem(gy + high, 2)
+    return to_x, to_y
 
 
 def exchange_kernel(
     state_hbm, vel_hbm, w_hbm, proj_hbm, diff_hbm, table_hbm, land_hbm, recv_hbm, ip_hbm,
     arrived, tracer, w_out, spread, recv_out, land_out,
-    ta, tb, vel, ex, buf, halo_out, halo_in, edge, wet, proj, land_row, diff, table, ip,
+    ta, tb, vel, ex, near, across, far_x, far_y, tab_in, buf,
+    halo_out, halo_in, edge, wet, proj, land_row, diff, table, tabs, ip,
     sem_state, sem_vel, sem_small, sem_w, sem_send, sem_recv, sem_hs, sem_hr,
+    sem_gs, sem_gr, sem_ts, sem_tr, sem_tabs,
 ):
     comp, gx, gy = lax.axis_index("comp"), lax.axis_index("gx"), lax.axis_index("gy")
     other = 1 - comp
@@ -73,9 +72,12 @@
     for i in range(S_PARTS):
         get_state(i).start()
     barrier = pltpu.get_barrier_semaphore()
-    for d in range(GROUP):
-        pl.semaphore_signal(barrier, inc=1, device_id=(other, d // N_GY, d % N_GY), device_id_type=MESH)
-    for device in beside:
+    peers = [(other, *place(gx, gy, dx, core, dy, high)) for dx, dy in STRAIGHT for core, high in EACH]
+    peers += [(other, *place(gx, gy, 0, core, dy, high)) for dy in range(4) for core, high in EACH]
+    peers += [(other, *place(gx, gy, dx, core, 0, high)) for dx in range(1, 4) for core, high in EACH]
+    peers += [(comp, *place(gx, gy, dx, core, dy, 0)) for dx, dy in VIA_Z for core in range(2) if dx or dy or core]
+    peers += [(comp, *place(gx, gy, 2, 0, 0, 0)), (comp, *place(gx, gy, 0, 0, 2, 0)), *beside]
+    for device in peers:
         pl.semaphore_signal(barrier, inc=1, device_id=device, device_id_type=MESH)
     for copy in small:
         copy.start()
@@ -101,35 +103,12 @@
             total = columns[0] * ta[0, pl.ds(TOP + x, 1), :]
             for l in range(1, LEV):
                 total += columns[l] * ta[l, pl.ds(TOP + x, 1), :]
-            ex[x] = total * jnp.where(comp == 0, 1.0, land_out[0, x].astype(F32))
+            ex[x] = (total * jnp.where(comp == 0, 1.0, land_out[0, x].astype(F32))).astype(BF16)
         return carry
 
     for i in range(S_PARTS):
         get_state(i).wait()
         lax.fori_loop(i * slab // 8, (i + 1) * slab // 8, export, 0)
-    pl.semaphore_wait(barrier, GROUP + 4)
-
-    def serve(turn, carry):
-        to_x, to_y = partner(turn, gx, gy)
-        d = to_x * N_GY + to_y
-        for q in range(CAP):
-            buf[turn * CAP + q] = ex[table[comp, q, d]].astype(BF16)
-        pltpu.make_async_remote_copy(
-            src_ref=buf.at[pl.ds(turn * CAP, CAP)],
-            dst_ref=arrived.at[pl.ds(me * CAP, CAP)],
-            send_sem=sem_send,
-            recv_sem=sem_recv,
-            device_id=(other, to_x, to_y),
-            device_id_type=MESH,
-        ).start()
-        return carry
-
-    def pick(l):
-        r = lax.broadcasted_iota(jnp.int32, (2 * LEV, TILE), 0)
-        c = lax.broadcasted_iota(jnp.int32, (2 * LEV, TILE), 1)
-        hit = ((r == l) & (c == 0)) | ((r == LEV + l) & (c == TILE - 1))
-        return jnp.where(hit, 1.0, 0.0).astype(BF16)
-
     r = lax.broadcasted_iota(jnp.int32, (FLD, TILE), 0)
     c = lax.broadcasted_iota(jnp.int32, (FLD, TILE), 1)
     both_ends = jnp.where(((r == 0) & (c == 0)) | ((r == 1) & (c == TILE - 1)), 1.0, 0.0).astype(BF16)
@@ -144,7 +123,7 @@
             device_id_type=MESH,
         )
 
-    def send_halo(turn, t):
+    def make_halo(turn, t):
         flat = t.reshape(LEV * PADDED, TILE)
         halo_out[turn, 0] = flat[pl.ds(TOP, LEV, stride=PADDED), :].astype(BF16)
         halo_out[turn, 1] = flat[pl.ds(TOP + ROWS - 1, LEV, stride=PADDED), :].astype(BF16)
@@ -157,6 +136,93 @@
             edge[1, l : l + 1, :] = ends[1:2]
         halo_out[turn, 2] = edge[0].astype(BF16)
         halo_out[turn, 3] = edge[1].astype(BF16)
+
+    make_halo(0, ta)
+    pl.semaphore_wait(barrier, len(peers))
+
+    far = lambda g: lax.rem(g + 4, 8)
+    gy_pair = lax.div(gy, 2) * 2
+    gy_twin = gy_pair + 1 - lax.rem(gy, 2)
+    relays = ((other, gx, gy), (other, gx, gy_twin), (comp, far(gx), gy), (comp, gx, far(gy)))
+    taken = (near, across, far_x, far_y)
+
+    def gather(i):
+        return pltpu.make_async_remote_copy(
+            src_ref=ex, dst_ref=taken[i], send_sem=sem_gs.at[i], recv_sem=sem_gr.at[i],
+            device_id=relays[i], device_id_type=MESH,
+        )
+
+    def gather_table(i):
+        return pltpu.make_async_remote_copy(
+            src_ref=table_hbm.at[comp], dst_ref=tab_in.at[i - 1], send_sem=sem_ts.at[i - 1], recv_sem=sem_tr.at[i - 1],
+            device_id=relays[i], device_id_type=MESH,
+        )
+
+    def fill(base, tiles, places, d):
+        for q in range(CAP):
+            buf[base + q] = tiles[places(q, d)]
+
+    def send(base, count, source, device):
+        pltpu.make_async_remote_copy(
+            src_ref=buf.at[pl.ds(base, count)],
+            dst_ref=arrived.at[pl.ds(source * CAP, count)],
+            send_sem=sem_send,
+            recv_sem=sem_recv,
+            device_id=device,
+            device_id_type=MESH,
+        ).start()
+
+    own_places = lambda q, d: table[comp, q, d]
+    near_places = lambda q, d: table[other, q, d]
+    across_places = lambda q, d: tabs[0, q, d]
+    far_x_places = lambda q, d: tabs[1, q, d]
+    far_y_places = lambda q, d: tabs[2, q, d]
+
+    def to_other(start, tiles, places, source, dx, dy):
+        def one(i, carry):
+            to_x, to_y = place(gx, gy, dx, lax.div(i, 2), dy, lax.rem(i, 2))
+            base = start + i * CAP
+            fill(base, tiles, places, to_x * N_GY + to_y)
+            send(base, CAP, source, (other, to_x, to_y))
+            return carry
+
+        lax.fori_loop(0, 4, one, 0)
+
+    def to_same(start, dx, dy):
+        first = 1 if dx == 0 and dy == 0 else 0
+
+        def one(i, carry):
+            to_x, to_y = place(gx, gy, dx, i, dy, 0)
+            base = start + (i - first) * SELF
+            d = to_x * N_GY + to_y
+            fill(base + lax.rem(gy, 2) * CAP, near, near_places, d)
+            fill(base + (1 - lax.rem(gy, 2)) * CAP, across, across_places, d)
+            send(base, SELF, gx * N_GY + gy_pair, (comp, to_x, to_y))
+            return carry
+
+        lax.fori_loop(first, 2, one, 0)
+
+    def keep():
+        for tiles, places, source in ((near, near_places, gy), (across, across_places, gy_twin)):
+            for q in range(CAP):
+                arrived[(gx * N_GY + source) * CAP + q] = tiles[places(q, me)]
+
+    for side in range(4):
+        halo_copy(0, side).start()
+    for i in range(1, 4):
+        gather_table(i).start()
+    for i in range(4):
+        gather(i).start()
+    for n, (dx, dy) in enumerate(STRAIGHT):
+        to_other(n * 4 * CAP, ex, own_places, me, dx, dy)
+
+    def pick(l):
+        r = lax.broadcasted_iota(jnp.int32, (2 * LEV, TILE), 0)
+        c = lax.broadcasted_iota(jnp.int32, (2 * LEV, TILE), 1)
+        hit = ((r == l) & (c == 0)) | ((r == LEV + l) & (c == TILE - 1))
+        return jnp.where(hit, 1.0, 0.0).astype(BF16)
+
+    def send_halo(turn):
         for side in range(4):
             halo_copy(turn, side).start()
 
@@ -195,18 +261,49 @@
     def put_tracer(l, value):
         tracer[l] = value
 
-    lax.fori_loop(0, FIRST, serve, 0)
     for copy in small[3:]:
         copy.wait()
     row_wet = jnp.where(comp == 0, jnp.ones((1, TILE), F32), land_row[...].astype(F32))
     wet[...] = jnp.transpose(jnp.broadcast_to(row_wet, (ROWS, TILE)))
-    send_halo(0, ta)
-    lax.fori_loop(FIRST, SECOND, serve, 0)
     edges = take_halo(0, ta)
     get_vel.wait()
     advance(ta, edges, put_tb)
-    send_halo(1, tb)
-    lax.fori_loop(SECOND, GROUP, serve, 0)
+    make_halo(1, tb)
+    send_halo(1)
+
+    for i in range(1, 4):
+        gather_table(i).wait_recv()
+    tabs_copy = pltpu.make_async_copy(tab_in, tabs, sem_tabs)
+    tabs_copy.start()
+    tabs_copy.wait()
+    for i in range(4):
+        gather(i).wait_recv()
+
+    x_source, y_source = far(gx) * N_GY + gy, gx * N_GY + far(gy)
+    four = 4 * CAP
+    base = 2 * four
+
+    def far_both(start):
+        @pl.when(lax.rem(gx, 2) == 0)
+        def _():
+            to_other(start, far_x, far_x_places, x_source, 0, 2)
+
+        @pl.when(lax.rem(gx, 2) == 1)
+        def _():
+            to_other(start, far_y, far_y_places, y_source, 2, 0)
+
+    steps = []
+    for n, (dx, dy) in enumerate(VIA_Z):
+        if n < len(NEAR):
+            steps.append((four, lambda at, k=NEAR[n]: to_other(at, far_x, far_x_places, x_source, 0, k)))
+            steps.append((four, lambda at, k=NEAR[n]: to_other(at, far_y, far_y_places, y_source, k, 0)))
+        elif n == len(NEAR):
+            steps.append((four, far_both))
+        steps.append((2 * SELF if dx or dy else SELF, lambda at, dx=dx, dy=dy: to_same(at, dx, dy)))
+    for count, step in steps:
+        step(base)
+        base += count
+    keep()
 
     def turn_w(i, carry):
         for j in range(TURNED):
@@ -226,8 +323,13 @@
     for turn in range(2):
         for side in range(4):
             halo_copy(turn, side).wait_send()
+    for i in range(1, 4):
+        gather_table(i).wait_send()
+    for i in range(4):
+        gather(i).wait_send()
     pltpu.make_async_copy(buf, buf, sem_send).wait()
-    pltpu.make_async_copy(arrived, arrived, sem_recv).wait()
+    others = arrived.at[pl.ds(0, GROUP * CAP - SELF)]
+    pltpu.make_async_copy(others, others, sem_recv).wait()
 
 
 def remap_kernel(recv, land, w, arrived, tracer, spread, new_hbm, imp_hbm, new, imp, sem_out):
@@ -287,8 +389,9 @@
             pltpu.VMEM((LEV, PADDED, TILE), F32),
             pltpu.VMEM((LEV, PADDED, TILE), F32),
             pltpu.VMEM((2, LEV, ROWS, TILE), BF16),
-            pltpu.VMEM((ROWS, FLD, TILE), F32),
-            pltpu.VMEM((GROUP * CAP, FLD, TILE), BF16),
+            *[pltpu.VMEM((ROWS, FLD, TILE), BF16) for _ in range(5)],
+            pltpu.VMEM((3, CAP, GROUP), jnp.int32),
+            pltpu.VMEM((GROUP * CAP - SELF, FLD, TILE), BF16),
             pltpu.VMEM((2, 4, LEV, TILE), BF16),
             pltpu.VMEM((2, 4, LEV, TILE), BF16),
             pltpu.VMEM((2, LEV, TILE), F32),
@@ -297,6 +400,7 @@
             pltpu.VMEM((1, ROWS), jnp.int32),
             pltpu.SMEM((1, LEV), F32),
             pltpu.SMEM((2, CAP, GROUP), jnp.int32),
+            pltpu.SMEM((3, CAP, GROUP), jnp.int32),
             pltpu.SMEM((FLD, LEV), F32),
             dma((S_PARTS,)),
             dma,
@@ -306,6 +410,11 @@
             dma,
             dma((2, 4)),
             dma((2, 4)),
+            dma((4,)),
+            dma((4,)),
+            dma((3,)),
+            dma((3,)),
+            dma,
         ],
         compiler_params=pltpu.CompilerParams(collective_id=0, has_side_effects=True, vmem_limit_bytes=16 << 20),
     )(*kept_in(pltpu.HBM, arrays))

time: 41.2 us -> 38.1 us (0.925)
  Pallas kernels: 40.5 us -> 37.4 us
    pallas_call x1, Pallas kernels: 36.5 us -> 33.4 us  [exchange(): pl.pallas_call(exchange_kernel, name='exchange', out_shape=(pltpu.VMEM((G...]
where the time goes in v5:
time: 38.1 us; the launch traced here: 38 us
  Pallas kernels  37.4 us (98%)
  between operations  0.64 us (2%)
    pallas_call x1, Pallas kernels, exchange(): pl.pallas_call(exchange_kernel, name='exchange', out_shape=(pltpu.VMEM((G...  33.4 us
    pallas_call x1, Pallas kernels, remap(): pl.pallas_call(remap_kernel, name='remap', out_shape=(jax.ShapeDtypeStruc...  4.03 us

profile of v5, /device:TPU:1, one launch (start us, length us, event | category | flops | bytes accessed | tf_op | source)
XLA Modules:
  0.0 38.0 jit_solution(5496367461187321940)
XLA Ops:
  0.6 33.4 %exchange.1 = (bf16[1024,8,128]{2,1,0:T(8,128)(2,1)S(1)}, f32[16,128,128]{2,1,0:T(8,128)S(1)}, bf16[128,4,128,128]{3,2,1,0:T(8,128)(2,1)S(1)}, f32[8,16,128]{2,1...) custom-call(f32[16,128,128]{2,1,0:T(8,128)} %bitcast.17, bf16[2,16,128,128]{3,2,1,0:T(8,128)(2,1)} %bitcast.18, ...), custom_call_target="tpu_custom_call" | custom-call | tf_op jit(solution)/shard_map/exchange/pallas_call | solution.py:375
  34.0 4.0 %remap.1 = (f32[16,128,128]{2,1,0:T(8,128)}, bf16[128,8,128]{2,1,0:T(8,128)(2,1)}) custom-call(s32[4,128]{1,0:T(4,128)S(4)} %get-tuple-element.10.recv, s32[1,128]{1,0:T(1,128)S(4)} %get-tuple-element.11.land, bf16[128,4,128,128]{3,2,1,0:T(8,128)(2,1)S(1)} %get-tuple-element.12.w, bf16[1024,8,128]{2,1,0:T(8,128)(2,1)S(1)} %get-tuple-element.13.arrived, ...), custom_call_target="tpu_custom_call" | custom-call | tf_op jit(solution)/shard_map/remap/pallas_call | solution.py:424

commit v6 on v5

--- a/solution.py
+++ b/solution.py
@@ -22,7 +22,7 @@
 SELF = 2 * CAP
 EACH = tuple((core, high) for core in range(2) for high in range(2))
 STRAIGHT = ((1, 1), (3, 3))
-VIA_Z = ((0, 1), (1, 0), (0, 3), (3, 0), (1, 3), (3, 1), (0, 0))
+VIA_Z = ((1, 3), (3, 1), (0, 1), (1, 0), (0, 3), (3, 0), (0, 0))
 NEAR = (0, 1, 3)
 
 
@@ -276,9 +276,6 @@
     tabs_copy = pltpu.make_async_copy(tab_in, tabs, sem_tabs)
     tabs_copy.start()
     tabs_copy.wait()
-    for i in range(4):
-        gather(i).wait_recv()
-
     x_source, y_source = far(gx) * N_GY + gy, gx * N_GY + far(gy)
     four = 4 * CAP
     base = 2 * four
@@ -292,15 +289,17 @@
         def _():
             to_other(start, far_y, far_y_places, y_source, 2, 0)
 
-    steps = []
-    for n, (dx, dy) in enumerate(VIA_Z):
-        if n < len(NEAR):
-            steps.append((four, lambda at, k=NEAR[n]: to_other(at, far_x, far_x_places, x_source, 0, k)))
-            steps.append((four, lambda at, k=NEAR[n]: to_other(at, far_y, far_y_places, y_source, k, 0)))
-        elif n == len(NEAR):
-            steps.append((four, far_both))
-        steps.append((2 * SELF if dx or dy else SELF, lambda at, dx=dx, dy=dy: to_same(at, dx, dy)))
-    for count, step in steps:
+    via_x = [(four, lambda at, k=k: to_other(at, far_x, far_x_places, x_source, 0, k)) for k in NEAR]
+    via_y = [(four, lambda at, k=k: to_other(at, far_y, far_y_places, y_source, k, 0)) for k in NEAR]
+    via_z = [
+        (2 * SELF if dx or dy else SELF, lambda at, dx=dx, dy=dy: to_same(at, dx, dy)) for dx, dy in VIA_Z
+    ]
+    both = [(four, far_both)]
+    rest = [via_x[1], via_y[1], via_x[2], via_y[2], *both, via_x[0], via_y[0]]
+    steps = [step for pair in zip(via_z, rest) for step in pair]
+    for n, (count, step) in enumerate(steps):
+        for i in {0: (0, 1), 1: (2,), 3: (3,)}.get(n, ()):
+            gather(i).wait_recv()
         step(base)
         base += count
     keep()

time: 38.1 us -> 37.4 us (0.982)
  Pallas kernels: 37.4 us -> 36.7 us
    pallas_call x1, Pallas kernels: 33.4 us -> 32.7 us  [exchange(): pl.pallas_call(exchange_kernel, name='exchange', out_shape=(pltpu.VMEM((G...]
where the time goes in v6:
time: 37.4 us; the launch traced here: 37.3 us
  Pallas kernels  36.7 us (98%)
  between operations  0.64 us (2%)
    pallas_call x1, Pallas kernels, exchange(): pl.pallas_call(exchange_kernel, name='exchange', out_shape=(pltpu.VMEM((G...  32.7 us
    pallas_call x1, Pallas kernels, remap(): pl.pallas_call(remap_kernel, name='remap', out_shape=(jax.ShapeDtypeStruc...  4.03 us

profile of v6, /device:TPU:1, one launch (start us, length us, event | category | flops | bytes accessed | tf_op | source)
XLA Modules:
  0.0 37.3 jit_solution(17014205811747057128)
XLA Ops:
  0.6 32.7 %exchange.1 = (bf16[1024,8,128]{2,1,0:T(8,128)(2,1)S(1)}, f32[16,128,128]{2,1,0:T(8,128)S(1)}, bf16[128,4,128,128]{3,2,1,0:T(8,128)(2,1)S(1)}, f32[8,16,128]{2,1...) custom-call(f32[16,128,128]{2,1,0:T(8,128)} %bitcast.17, bf16[2,16,128,128]{3,2,1,0:T(8,128)(2,1)} %bitcast.18, ...), custom_call_target="tpu_custom_call" | custom-call | tf_op jit(solution)/shard_map/exchange/pallas_call | solution.py:374
  33.3 4.0 %remap.1 = (f32[16,128,128]{2,1,0:T(8,128)}, bf16[128,8,128]{2,1,0:T(8,128)(2,1)}) custom-call(s32[4,128]{1,0:T(4,128)S(4)} %get-tuple-element.10.recv, s32[1,128]{1,0:T(1,128)S(4)} %get-tuple-element.11.land, bf16[128,4,128,128]{3,2,1,0:T(8,128)(2,1)S(1)} %get-tuple-element.12.w, bf16[1024,8,128]{2,1,0:T(8,128)(2,1)S(1)} %get-tuple-element.13.arrived, ...), custom_call_target="tpu_custom_call" | custom-call | tf_op jit(solution)/shard_map/remap/pallas_call | solution.py:423

commit v7 on v6

--- a/solution.py
+++ b/solution.py
@@ -211,7 +211,7 @@
         halo_copy(0, side).start()
     for i in range(1, 4):
         gather_table(i).start()
-    for i in range(4):
+    for i in (2, 3, 0, 1):
         gather(i).start()
     for n, (dx, dy) in enumerate(STRAIGHT):
         to_other(n * 4 * CAP, ex, own_places, me, dx, dy)

time: 37.4 us -> 37.4 us (level)
  no operation moved by 1% of the time
where the time goes in v7:
time: 37.4 us; the launch traced here: 37.3 us
  Pallas kernels  36.7 us (98%)
  between operations  0.64 us (2%)
    pallas_call x1, Pallas kernels, exchange(): pl.pallas_call(exchange_kernel, name='exchange', out_shape=(pltpu.VMEM((G...  32.7 us
    pallas_call x1, Pallas kernels, remap(): pl.pallas_call(remap_kernel, name='remap', out_shape=(jax.ShapeDtypeStruc...  4.02 us

profile of v7, /device:TPU:1, one launch (start us, length us, event | category | flops | bytes accessed | tf_op | source)
XLA Modules:
  0.0 37.3 jit_solution(14452131037485435090)
XLA Ops:
  0.6 32.7 %exchange.1 = (bf16[1024,8,128]{2,1,0:T(8,128)(2,1)S(1)}, f32[16,128,128]{2,1,0:T(8,128)S(1)}, bf16[128,4,128,128]{3,2,1,0:T(8,128)(2,1)S(1)}, f32[8,16,128]{2,1...) custom-call(f32[16,128,128]{2,1,0:T(8,128)} %bitcast.17, bf16[2,16,128,128]{3,2,1,0:T(8,128)(2,1)} %bitcast.18, ...), custom_call_target="tpu_custom_call" | custom-call | tf_op jit(solution)/shard_map/exchange/pallas_call | solution.py:374
  33.3 4.0 %remap.1 = (f32[16,128,128]{2,1,0:T(8,128)}, bf16[128,8,128]{2,1,0:T(8,128)(2,1)}) custom-call(s32[4,128]{1,0:T(4,128)S(4)} %get-tuple-element.10.recv, s32[1,128]{1,0:T(1,128)S(4)} %get-tuple-element.11.land, bf16[128,4,128,128]{3,2,1,0:T(8,128)(2,1)S(1)} %get-tuple-element.12.w, bf16[1024,8,128]{2,1,0:T(8,128)(2,1)S(1)} %get-tuple-element.13.arrived, ...), custom_call_target="tpu_custom_call" | custom-call | tf_op jit(solution)/shard_map/remap/pallas_call | solution.py:423
